TPU v7x, 512 devices: a whole 4x4x16 slice. The times are simulated.
512 devices in a mesh: mem: 8 (over x, core), space: 64 (over z, y).
Axes of the slice: x: 4, y: 4, z: 16, core: 2. Of those that a mesh axis runs over, the one named last changes fastest.
Arguments:
- ensemble: float32 [80, 8, 256, 640], P('mem', None, 'space'), may hold values from -6 to 6
- diffusivity: float32 [256, 640], P('space'), may hold values from 0.04 to 0.2
- obs_row: int32 [256], replicated, may hold values from 0 to 255
- obs_lon: int32 [256], replicated, may hold values from 0 to 639
- obs_level: int32 [256], replicated, may hold values from 0 to 7
- obs_order: int32 [256], replicated, may hold values from 0 to 255, each once
- obs_value: float32 [256], replicated, may hold values from -6 to 6
- obs_error: float32 [256], replicated, may hold values from 0.1 to 2
- coupling: float32 [8, 8], replicated, may hold values from 0.3 to 1
Outputs:
- analysis: float32 [80, 8, 256, 640], P(None, 'mem', 'space')
All inputs are finite; a program needn't handle non-finite values.
Results may differ from a plain program's by a relative error of at most 0.00011.
Values sent between devices are 32-bit elements; how exact they have to be, the bound alone decides.
No kernel may reach another device: no remote copies, remote signals or barrier semaphores. Data moves between devices by JAX's collectives and lax.ppermute only.
A program may use at most 64 MiB of HBM per device.

v0:
```python
import jax
import jax.numpy as jnp
from jax import lax
from jax.sharding import PartitionSpec as P

V = 4
OBS_BLOCK = 128
BLOCKS = 2
LOC_RADIUS = 16


ADVECT = 0.15


def padded_2(block, sides, width):
    for axis, dim in sides:
        count = lax.axis_size(axis)
        forward = [(i, i + 1) for i in range(count - 1)]
        backward = [(target, source) for source, target in forward]
        low = lax.ppermute(
            lax.slice_in_dim(block, block.shape[dim] - width, None, axis=dim), axis, forward
        )
        high = lax.ppermute(lax.slice_in_dim(block, 0, width, axis=dim), axis, backward)
        block = jnp.concatenate([low, block, high], axis=dim)
    return block


def advance(padded, diff):
    centre = padded[..., 1:-1, :]
    north = padded[..., 2:, :]
    south = padded[..., :-2, :]
    east = jnp.roll(centre, -1, axis=-1)
    west = jnp.roll(centre, 1, axis=-1)
    lead = centre.shape[:-3]
    rows = centre.shape[-2]
    width = centre.shape[-1]

    def grouped(field):
        return field.reshape(lead + (V, field.shape[-3] // V, rows, width))

    here, right, left, upper, lower = (
        grouped(centre),
        grouped(east),
        grouped(west),
        grouped(north),
        grouped(south),
    )
    wind_u = here[..., 0:1, :, :, :]
    wind_w = here[..., 1:2, :, :, :]
    moved = here - ADVECT * (wind_u * (right - left) + wind_w * (upper - lower))
    moved = moved + diff * (right + left + upper + lower - 4.0 * here)
    return moved.reshape(centre.shape)


def adjust(prior, values, errors):
    members = prior.shape[0]
    mean = jnp.mean(prior, axis=0)
    dev = prior - mean
    var = jnp.sum(dev * dev, axis=0) / (members - 1) + 1e-06
    post_var = 1.0 / (1.0 / var + 1.0 / errors)
    post_mean = post_var * (mean / var + values / errors)
    shrink = jnp.sqrt(errors / (errors + var))
    incr = post_mean + shrink * dev - prior
    gain = dev / ((members - 1) * var)
    return (incr, gain)


def spread_weights(cell_rows, cell_lons, rows, lons, width, radius):
    dist_rows = jnp.abs(cell_rows[None, :, None] - rows[:, None, None])
    dist_lons = jnp.abs(cell_lons[None, None, :] - lons[:, None, None])
    dist_lons = jnp.minimum(dist_lons, width - dist_lons)
    dist = (dist_rows + dist_lons).astype(jnp.float32)
    near = jnp.maximum(jnp.float32(0.0), 1.0 - dist / radius)
    return near * near


def shards(
    ensemble, diffusivity, obs_row, obs_lon, obs_level, obs_order, obs_value, obs_error, coupling
):
    tile_rows = ensemble.shape[2]
    width = ensemble.shape[3]
    tile_start = lax.axis_index("space") * tile_rows
    field = ensemble
    for sub in range(2):
        padded = padded_2(field, (("space", 2),), 1)
        field = advance(padded, diffusivity)
    state = lax.all_to_all(field, "mem", split_axis=1, concat_axis=0, tiled=True)
    members, own_levels = (state.shape[0], state.shape[1])
    level_start = lax.axis_index("mem") * own_levels
    flat_state = state.reshape(members, -1)
    cell_rows = tile_start + jnp.arange(tile_rows, dtype=jnp.int32)
    cell_lons = jnp.arange(width, dtype=jnp.int32)
    for block in range(BLOCKS):
        pick = obs_order[block * OBS_BLOCK : (block + 1) * OBS_BLOCK]
        rows = obs_row[pick]
        lons = obs_lon[pick]
        levs = obs_level[pick]
        local_level = levs - level_start
        local_row = rows - tile_start
        owned = (
            (local_level >= 0)
            & (local_level < own_levels)
            & (local_row >= 0)
            & (local_row < tile_rows)
        )
        flat_index = (
            jnp.clip(local_level, 0, own_levels - 1) * tile_rows
            + jnp.clip(local_row, 0, tile_rows - 1)
        ) * width + lons
        picked = jnp.take(flat_state, flat_index, axis=1)
        local_prior = jnp.where(owned[None, :], picked, jnp.float32(0.0))
        prior = lax.psum(local_prior, ("mem", "space"))
        incr, gain = adjust(prior, obs_value[pick], obs_error[pick])
        spatial = spread_weights(cell_rows, cell_lons, rows, lons, width, float(LOC_RADIUS))
        couple = lax.dynamic_slice_in_dim(coupling[levs], level_start, own_levels, axis=1)
        weights = (couple[:, :, None, None] * spatial[:, None, :, :]).reshape(OBS_BLOCK, -1)
        coef = jnp.dot(gain.T, flat_state, precision=lax.Precision.HIGHEST)
        flat_state = flat_state + jnp.dot(incr, weights * coef, precision=lax.Precision.HIGHEST)
    return flat_state.reshape(state.shape)


def solution(mesh):
    placed = (P("mem", None, "space", None), P("space", None), P(), P(), P(), P(), P(), P(), P())
    return jax.shard_map(
        shards, mesh=mesh, in_specs=placed, out_specs=P(None, "mem", "space", None), check_vma=False
    )
```

profile of v0, /device:TPU:1, one launch (start us, length us, event | category | flops | bytes accessed | tf_op | source)
XLA Modules:
  0.0 308.9 jit_solution(17932524736407729049)
XLA Ops:
  2.0 1.3 collective-permute-start
  3.3 5.5 %collective-permute-start.1 = (f32[10,8,1,640]{3,1,2,0:T(8,128)}, f32[10,8,1,640]{3,1,2,0:T(8,128)}, u32[]{:S(2)}, u32[]{:S(2)}) collective-permute-start(f32[10,8,1,640]{3,1,2,0:T(8,128)} %get-tuple-element.27), channel_id=1, source_target_pairs={{0,1},{1,2},{2,3},{3,4},{4,5},{5,6},{6,7},{7,8},{8,9},{9,10},{10,1... | collective-permute-start | bytes 614408 | tf_op jit(solution)/shard_map/ppermute | solution.py:20
  8.8 1.4 fusion.33
  10.3 1.3 gather_fusion
  11.6 1.3 gather_fusion.1
  12.9 1.3 gather_fusion.6
  14.2 1.3 gather_fusion.7
  15.4 1.3 gather_fusion.2
  18.4 1.5 mul.210
  20.2 1.5 mul.214
  22.3 1.7 maximum_multiply_fusion.1
  25.3 3.3 %multiply_add_fusion.2 = (f32[10,8,4,640]{3,1,2,0:T(8,128)S(1)}, f32[10,8,4,640]{3,1,2,0:T(8,128)}, f32[10,8,4,640]{3,1,2,0:T(8,128)}, f32[10,8,4,640]{3,1,2,0:T(8,128)}, f32[10,8,4,640]{3,1,2,0:T(8,128)}) fusion(f32[10,8,4,640]{3,1,2,0:T(8,128)S(1)} %copy.46, f32[10,8,4,640]{3,1,2,0:T(8,128)S(1)} %copy-done.15, f32[10,8,4,640]{3,1,2,0:T(8,128)S(1)} %copy-done.13, ...), kind=kLoop, calls=%fused_computation.30 | loop fusion | flops 3686400 | bytes 8611840 | tf_op jit(solution)/shard_map/add | solution.py:51
  28.7 1.4 fusion.30
  30.9 2.5 add.254
  33.4 1.4 reshape.305
  34.8 2.6 reshape.306
  37.4 2.5 sub.209
  39.9 2.9 multiply_add_fusion.1
  43.1 1.5 mul.228
  45.7 2.7 mul.232
  48.4 1.3 collective-permute-start.2
  49.7 4.2 %collective-permute-start.3 = (f32[10,8,1,640]{3,1,2,0:T(8,128)S(1)}, f32[10,8,1,640]{3,1,2,0:T(8,128)S(1)}, u32[]{:S(2)}, u32[]{:S(2)}) collective-permute-start(f32[10,8,1,640]{3,1,2,0:T(8,128)S(1)} %copy-done.17), channel_id=1, source_target_pairs={{0,1},{1,2},{2,3},{3,4},{4,5},{5,6},{6,7},{7,8},{8,9},{9,10},{10,1... | collective-permute-start | bytes 614408 | tf_op jit(solution)/shard_map/ppermute | solution.py:20
  54.8 1.5 collective-permute-done.3
  56.3 2.3 multiply_add_fusion
  59.7 11.5 %all-to-all-start = ((f32[10,8,4,640]{3,2,0,1:T(4,128)}), f32[10,8,4,640]{3,2,0,1:T(4,128)S(1)}, u32[]{:S(2)}, u32[]{:S(2)}) async-start(f32[10,8,4,640]{3,2,0,1:T(4,128)} %copy.50), calls=%async_computation | async-start | bytes 1638400 | tf_op jit(solution)/shard_map/all_to_all | solution.py:87
  80.9 3.0 all-to-all-done
  85.1 111.7 %psum.14 = f32[80,128]{0,1:T(8,128)S(1)} all-reduce(f32[80,128]{0,1:T(8,128)S(1)} %bitcast_select_fusion.1), channel_id=1, replica_groups=mesh['mem'=8,'space'=64] {'mem','space'}, use_global_device_ids=true, to_apply=%region_0.2 | all-reduce | flops 10240 | bytes 81920 | tf_op jit(solution)/shard_map/psum | solution.py:112
  197.1 1.9 convolution_multiply_fusion.1
  200.0 1.5 copy.53
  201.5 2.0 gather_fusion.13
  203.6 101.5 %psum.15 = f32[80,128]{0,1:T(8,128)S(1)} all-reduce(f32[80,128]{0,1:T(8,128)S(1)} %bitcast_select_fusion), channel_id=1, replica_groups=mesh['mem'=8,'space'=64] {'mem','space'}, use_global_device_ids=true, to_apply=%region_3.5 | all-reduce | flops 10240 | bytes 81920 | tf_op jit(solution)/shard_map/psum | solution.py:112
  305.4 1.3 convolution_multiply_fusion
  (103 shorter events, 24.9 us)
Async XLA Ops:
  0.0 77.5 %copy-start = (f32[8,8]{1,0:T(8,128)S(1)}, f32[8,8]{1,0:T(8,128)}, u32[]{:S(2)}) copy-start(f32[8,8]{1,0:T(8,128)} %param.19) | copy-start | bytes 772
  2.0 22.6 %collective-permute-start = (f32[10,8,1,640]{3,1,2,0:T(8,128)}, f32[10,8,1,640]{3,1,2,0:T(8,128)}, u32[]{:S(2)}, u32[]{:S(2)}) collective-permute-start(f32[10,8,1,640]{3,1,2,0:T(8,128)} %get-tuple-element.28), channel_id=1, source_target_pairs={{1,0},{2,1},{3,2},{4,3},{5,4},{6,5},{7,6},{8,7},{9,8},{10,9},{11,1... | collective-permute-start | bytes 614408 | tf_op jit(solution)/shard_map/ppermute | solution.py:23
  3.3 7.0 %copy-start.20 = (s32[256]{0:T(256)S(1)}, s32[256]{0:T(256)}, u32[]{:S(2)}) copy-start(s32[256]{0:T(256)} %param.16) | copy-start | bytes 3076
  3.3 7.0 %copy-start.1 = (s32[256]{0:T(256)S(1)}, s32[256]{0:T(256)}, u32[]{:S(2)}) copy-start(s32[256]{0:T(256)} %param.15) | copy-start | bytes 3076
  3.3 8.3 %copy-start.2 = (s32[256]{0:T(256)S(1)}, s32[256]{0:T(256)}, u32[]{:S(2)}) copy-start(s32[256]{0:T(256)} %param.13) | copy-start | bytes 3076
  3.3 21.3 %collective-permute-start.1 = (f32[10,8,1,640]{3,1,2,0:T(8,128)}, f32[10,8,1,640]{3,1,2,0:T(8,128)}, u32[]{:S(2)}, u32[]{:S(2)}) collective-permute-start(f32[10,8,1,640]{3,1,2,0:T(8,128)} %get-tuple-element.27), channel_id=1, source_target_pairs={{0,1},{1,2},{2,3},{3,4},{4,5},{5,6},{6,7},{7,8},{8,9},{9,10},{10,1... | collective-permute-start | bytes 614408 | tf_op jit(solution)/shard_map/ppermute | solution.py:20
  10.3 5.2 %copy-start.3 = (s32[256]{0:T(256)S(1)}, s32[256]{0:T(256)}, u32[]{:S(2)}) copy-start(s32[256]{0:T(256)} %param.14) | copy-start | bytes 3076
  11.6 6.4 %copy-start.9 = (f32[10,8,4,640]{3,2,1,0:T(4,128)S(1)}, f32[10,8,4,640]{3,2,1,0:T(4,128)}, u32[]{:S(2)}) copy-start(f32[10,8,4,640]{3,2,1,0:T(4,128)} %param.11) | copy-start | bytes 2457604
  22.3 2.4 copy-start.13
  22.3 2.4 copy-start.15
  23.9 1.1 copy-start.11
  23.9 1.4 copy-start.12
  23.9 1.4 copy-start.19
  30.1 3.3 %copy-start.16 = (f32[10,8,4,640]{3,1,2,0:T(8,128)S(1)}, f32[10,8,4,640]{3,1,2,0:T(8,128)}, u32[]{:S(2)}) copy-start(f32[10,8,4,640]{3,1,2,0:T(8,128)} %get-tuple-element.13) | copy-start | bytes 2457604
  34.8 5.1 %copy-start.10 = (f32[10,8,4,640]{3,2,1,0:T(4,128)S(1)}, f32[10,8,4,640]{3,2,1,0:T(4,128)}, u32[]{:S(2)}) copy-start(f32[10,8,4,640]{3,2,1,0:T(4,128)} %param.11) | copy-start | bytes 2457604
  44.6 5.1 %copy-start.17 = (f32[10,8,1,640]{3,1,2,0:T(8,128)S(1)}, f32[10,8,1,640]{3,1,2,0:T(8,128)}, u32[]{:S(2)}) copy-start(f32[10,8,1,640]{3,1,2,0:T(8,128)} %get-tuple-element.21) | copy-start | bytes 614404
  45.7 2.7 copy-start.18
  45.7 10.7 %copy-start.14 = (f32[10,8,4,639]{3,1,2,0:T(8,128)S(1)}, f32[10,8,4,639]{3,1,2,0:T(8,128)}, u32[]{:S(2)}) copy-start(f32[10,8,4,639]{3,1,2,0:T(8,128)} %get-tuple-element.15) | copy-start | bytes 2453764
  48.4 6.5 %collective-permute-start.2 = (f32[10,8,1,640]{3,1,2,0:T(8,128)S(1)}, f32[10,8,1,640]{3,1,2,0:T(8,128)S(1)}, u32[]{:S(2)}, u32[]{:S(2)}) collective-permute-start(f32[10,8,1,640]{3,1,2,0:T(8,128)S(1)} %copy-done.18), channel_id=1, source_target_pairs={{1,0},{2,1},{3,2},{4,3},{5,4},{6,5},{7,6},{8,7},{9,8},{10,9},{11,1... | collective-permute-start | bytes 614408 | tf_op jit(solution)/shard_map/ppermute | solution.py:23
  49.7 6.7 %collective-permute-start.3 = (f32[10,8,1,640]{3,1,2,0:T(8,128)S(1)}, f32[10,8,1,640]{3,1,2,0:T(8,128)S(1)}, u32[]{:S(2)}, u32[]{:S(2)}) collective-permute-start(f32[10,8,1,640]{3,1,2,0:T(8,128)S(1)} %copy-done.17), channel_id=1, source_target_pairs={{0,1},{1,2},{2,3},{3,4},{4,5},{5,6},{6,7},{7,8},{8,9},{9,10},{10,1... | collective-permute-start | bytes 614408 | tf_op jit(solution)/shard_map/ppermute | solution.py:20
  58.6 12.6 %copy-start.4 = (f32[256]{0:T(256)S(1)}, f32[256]{0:T(256)}, u32[]{:S(2)}) copy-start(f32[256]{0:T(256)} %param.18) | copy-start | bytes 3076
  59.7 14.1 %copy-start.5 = (f32[256]{0:T(256)S(1)}, f32[256]{0:T(256)}, u32[]{:S(2)}) copy-start(f32[256]{0:T(256)} %param.17) | copy-start | bytes 3076
  59.7 24.1 %all-to-all-start = ((f32[10,8,4,640]{3,2,0,1:T(4,128)}), f32[10,8,4,640]{3,2,0,1:T(4,128)S(1)}, u32[]{:S(2)}, u32[]{:S(2)}) async-start(f32[10,8,4,640]{3,2,0,1:T(4,128)} %copy.50), calls=%async_computation | async-start | bytes 1638400 | tf_op jit(solution)/shard_map/all_to_all | solution.py:87
  71.2 5.1 %copy-start.6 = (f32[128,4,640]{2,1,0:T(4,128)S(1)}, f32[128,4,640]{2,1,0:T(4,128)}, u32[]{:S(2)}) copy-start(f32[128,4,640]{2,1,0:T(4,128)} %maximum_multiply_fusion.1) | copy-start | bytes 3932164
  83.9 113.2 %copy-start.8 = (f32[16,8,4,640]{3,1,2,0:T(8,128)S(1)}, f32[16,8,4,640]{3,1,2,0:T(8,128)}, u32[]{:S(2)}) copy-start(f32[16,8,4,640]{3,1,2,0:T(8,128)} %copy.57) | copy-start | bytes 3932164
  200.0 105.4 %copy-start.7 = (f32[16,8,4,640]{3,1,2,0:T(8,128)S(1)}, f32[16,8,4,640]{3,1,2,0:T(8,128)}, u32[]{:S(2)}) copy-start(f32[16,8,4,640]{3,1,2,0:T(8,128)} %copy.58) | copy-start | bytes 3932164
where the time goes:
time: 310 us; the launch traced here: 309 us
  blocking collectives  213 us (69%)
  local copies, waits for them, and re-layouts  49 us (16%)
  starting transfers between devices  23.7 us (8%)
  other arithmetic  11.9 us (4%)
  waiting for transfers between devices  5.34 us (2%)
  matrix products  5.15 us (2%)
    psum x2, blocking collectives, shards(): prior = lax.psum(local_prior, ('mem', 'space'))  213 us
    all_to_all x1, starting transfers between devices, shards(): lax.all_to_all(field, 'mem', split_axis=1, concat_axis=0, tiled=True)  11.5 us
    ppermute x2, starting transfers between devices, padded_2(): lax.ppermute(lax.slice_in_dim(block, block.shape[dim] - width, None, axis...  9.66 us
    mul x12, local copies, waits for them, and re-layouts, advance(): moved = here - ADVECT * (wind_u * (right - left) + wind_w * (upper - lower))  9.09 us
    add x3, other arithmetic, advance(): moved = moved + diff * (right + left + upper + lower - 4.0 * here)  8.46 us
  transfers between devices with their start and end apart: 5, of which 3 were waited for; matrix products, arithmetic and copies ran while one was open for 8% of the time, Pallas kernels for 0%

commit v1 on v0

v1 whole, which is shorter than its diff:
```python
import jax
import jax.numpy as jnp
from jax import lax
from jax.experimental import pallas as pl
from jax.experimental.pallas import tpu as pltpu
from jax.sharding import Mesh
from jax.sharding import PartitionSpec as P

V = 4
OBS_BLOCK = 128
LOC_RADIUS = 16
ADVECT = 0.15
HALO = 2
LANES = 128
FULL = lax.Precision.HIGHEST


def vmem_specs(count):
    return [pl.BlockSpec(memory_space=pltpu.VMEM)] * count


def params():
    return pltpu.CompilerParams(vmem_limit_bytes=48 * 1024 * 1024)


def prepare(tile_rows, width, place_ref, row_ref, lon_ref, lev_ref, order_ref, value_ref, error_ref,
            coupling_ref, fields_ref, weight_ref, cross_ref, onehot_ref, pick_ref):
    count = row_ref.shape[1]
    levels = coupling_ref.shape[0]
    tile_start = place_ref[0]
    own_level = place_ref[1]
    fields = jnp.concatenate(
        [
            row_ref[...].astype(jnp.float32),
            lon_ref[...].astype(jnp.float32),
            lev_ref[...].astype(jnp.float32),
            value_ref[...],
            error_ref[...],
            jnp.zeros((3, count), jnp.float32),
        ],
        axis=0,
    )
    source = lax.broadcasted_iota(jnp.int32, (count, count), 0)
    taken = (source == order_ref[...]).astype(jnp.float32)
    ordered = jnp.dot(fields, taken, precision=FULL, preferred_element_type=jnp.float32)
    fields_ref[...] = ordered
    rows = ordered[0:1]
    lons = ordered[1:2]
    levs = ordered[2:3]
    columns = jnp.concatenate([ordered, jnp.zeros((LANES - 8, count), jnp.float32)], axis=0).T
    row_col = columns[:, 0:1]
    lon_col = columns[:, 1:2]
    lev_col = columns[:, 2:3]

    def near(drow, dlon):
        dlon = jnp.minimum(dlon, width - dlon)
        close = jnp.maximum(0.0, 1.0 - (drow + dlon) / LOC_RADIUS)
        return close * close

    coupled = jnp.zeros((count, levels), jnp.float32)
    coupled_own = jnp.zeros((count, 1), jnp.float32)
    table = coupling_ref[...]
    lane = lax.broadcasted_iota(jnp.int32, (levels, levels), 1)
    own = jnp.sum(jnp.where(lane == own_level, table, 0.0), axis=1, keepdims=True)
    for level in range(levels):
        here = lev_col == level
        coupled = jnp.where(here, table[level:level + 1, :], coupled)
        coupled_own = jnp.where(here, own[level:level + 1, :], coupled_own)
    cell_lon = lax.broadcasted_iota(jnp.int32, (1, width), 1).astype(jnp.float32)
    dlon = jnp.abs(cell_lon - lon_col)
    for row in range(tile_rows):
        drow = jnp.abs((tile_start + row).astype(jnp.float32) - row_col)
        weight_ref[row] = coupled_own * near(drow, dlon)

    first = slice(0, OBS_BLOCK)
    second = slice(OBS_BLOCK, 2 * OBS_BLOCK)
    between = jnp.zeros((OBS_BLOCK, OBS_BLOCK), jnp.float32)
    for level in range(levels):
        between = jnp.where(levs[:, second] == level, coupled[first, level:level + 1], between)
    cross_ref[...] = between * near(
        jnp.abs(row_col[first] - rows[:, second]), jnp.abs(lon_col[first] - lons[:, second])
    )

    lon_id = lax.broadcasted_iota(jnp.int32, (width, count), 0).astype(jnp.float32)
    onehot_ref[...] = (lon_id == lons).astype(jnp.bfloat16)
    slot = lax.broadcasted_iota(jnp.int32, (8, count), 0).astype(jnp.float32)
    local = rows - tile_start.astype(jnp.float32) + HALO
    inside = (slot == local) & (slot >= HALO) & (slot < HALO + tile_rows)
    for level in range(levels):
        pick_ref[level] = jnp.where(inside & (levs == level), 1.0, 0.0)


def forecast(x_ref, low_ref, high_ref, diff_ref, onehot_ref, pick_ref, out_ref, prior_ref, wide_ref):
    members, levels, tile_rows, width = x_ref.shape
    deep = tile_rows + 2 * HALO
    heights = levels // V
    extra = members * levels
    diff = jnp.concatenate([low_ref[extra], diff_ref[...], high_ref[extra]], axis=0)

    def sub_step(fields):
        wind_u, wind_w = fields[0], fields[1]
        moved = []
        for q in fields:
            east = pltpu.roll(q, width - 1, 1)
            west = pltpu.roll(q, 1, 1)
            north = pltpu.roll(q, deep - 1, 0)
            south = pltpu.roll(q, 1, 0)
            new = q - ADVECT * (wind_u * (east - west) + wind_w * (north - south))
            moved.append(new + diff * (east + west + north + south - 4.0 * q))
        return moved

    @pl.loop(0, members)
    def _(member):
        for height in range(heights):
            fields = []
            for v in range(V):
                level = v * heights + height
                at = member * levels + level
                fields.append(
                    jnp.concatenate([low_ref[at], x_ref[member, level], high_ref[at]], axis=0)
                )
            fields = sub_step(sub_step(fields))
            for v in range(V):
                level = v * heights + height
                out_ref[level, member] = fields[v][HALO:HALO + tile_rows]
                wide_ref[level, member] = fields[v]

    def gather(level, total):
        rest = wide_ref[level].reshape(members * deep, width)
        found = jnp.zeros((members * deep, onehot_ref.shape[1]), jnp.float32)
        for _ in range(3):
            part = rest.astype(jnp.bfloat16)
            rest = rest - part.astype(jnp.float32)
            found = found + jnp.dot(part, onehot_ref[...], preferred_element_type=jnp.float32)
        return total + found.reshape(members, deep, -1) * pick_ref[level][None]

    total = lax.fori_loop(
        0, levels, gather, jnp.zeros((members, deep, onehot_ref.shape[1]), jnp.float32)
    )
    prior_ref[...] = jnp.sum(total, axis=1)


def adjust(prior, values, errors):
    members = prior.shape[0]
    mean = jnp.sum(prior, axis=0, keepdims=True) / members
    dev = prior - mean
    var = jnp.sum(dev * dev, axis=0, keepdims=True) / (members - 1) + 1e-06
    post_var = 1.0 / (1.0 / var + 1.0 / errors)
    post_mean = post_var * (mean / var + values / errors)
    shrink = jnp.sqrt(errors / (errors + var))
    incr = post_mean + shrink * dev - prior
    gain = dev / ((members - 1) * var)
    return incr, gain.T


def dot(a, b):
    return jnp.dot(a, b, precision=FULL, preferred_element_type=jnp.float32)


def analyse(x_ref, prior_ref, fields_ref, weight_ref, cross_ref, out_ref):
    members, tile_rows, _ = x_ref.shape
    planes, tiles, share, _ = prior_ref.shape
    prior = jnp.concatenate(
        [sum(prior_ref[i, t] for t in range(tiles)) for i in range(planes)], axis=0
    )
    values = fields_ref[3:4]
    errors = fields_ref[4:5]
    first = slice(0, OBS_BLOCK)
    second = slice(OBS_BLOCK, 2 * OBS_BLOCK)
    incr0, gain0 = adjust(prior[:, first], values[:, first], errors[:, first])
    later = prior[:, second]
    later = later + dot(incr0, cross_ref[...] * dot(gain0, later))
    incr1, gain1 = adjust(later, values[:, second], errors[:, second])
    for row in range(tile_rows):
        x = x_ref[:, row, :]
        x = x + dot(incr0, weight_ref[row, first, :] * dot(gain0, x))
        x = x + dot(incr1, weight_ref[row, second, :] * dot(gain1, x))
        out_ref[:, row, :] = x


def shards(ensemble, diffusivity, obs_row, obs_lon, obs_level, obs_order, obs_value, obs_error, coupling):
    members, levels, tile_rows, width = ensemble.shape
    count = obs_row.shape[0]
    space = ("z", "y")
    mem = ("x", "core")
    tiles = lax.axis_size(space)
    planes = lax.axis_size("z")
    own_level = lax.axis_index(mem)
    place = jnp.stack([lax.axis_index(space) * tile_rows, own_level]).astype(jnp.int32)

    flat = ensemble.reshape(members * levels, tile_rows, width)
    edges = jnp.concatenate([flat, diffusivity[None]], axis=0)
    low = lax.ppermute(edges[:, tile_rows - HALO:], space, [(i, i + 1) for i in range(tiles - 1)])
    high = lax.ppermute(edges[:, :HALO], space, [(i + 1, i) for i in range(tiles - 1)])

    line = lambda a: a.reshape(1, count)
    fields, weight, cross, onehot, pick = pl.pallas_call(
        lambda *refs: prepare(tile_rows, width, *refs),
        out_shape=[
            jax.ShapeDtypeStruct((8, count), jnp.float32),
            jax.ShapeDtypeStruct((tile_rows, count, width), jnp.float32),
            jax.ShapeDtypeStruct((OBS_BLOCK, OBS_BLOCK), jnp.float32),
            jax.ShapeDtypeStruct((width, count), jnp.bfloat16),
            jax.ShapeDtypeStruct((levels, 8, count), jnp.float32),
        ],
        in_specs=[pl.BlockSpec(memory_space=pltpu.SMEM)] + vmem_specs(7),
        out_specs=vmem_specs(5),
        compiler_params=params(),
        cost_estimate=pl.CostEstimate(flops=10_000_000, bytes_accessed=4_000_000, transcendentals=0),
        name="prepare",
    )(place, line(obs_row), line(obs_lon), line(obs_level), line(obs_order), line(obs_value),
      line(obs_error), coupling)

    state, prior = pl.pallas_call(
        forecast,
        out_shape=[
            jax.ShapeDtypeStruct((levels, members, tile_rows, width), jnp.float32),
            jax.ShapeDtypeStruct((members, count), jnp.float32),
        ],
        in_specs=vmem_specs(6),
        out_specs=vmem_specs(2),
        scratch_shapes=[pltpu.VMEM((levels, members, tile_rows + 2 * HALO, width), jnp.float32)],
        compiler_params=params(),
        name="forecast",
    )(ensemble, low, high, diffusivity, onehot, pick)

    reach = 2 * (LOC_RADIUS - 1)
    tiles_reached = -(-reach // tile_rows)
    rows_of_tiles = tiles // planes
    planes_reached = min(-(-tiles_reached // rows_of_tiles), planes - 1)
    near = prior
    for d in range(1, planes_reached + 1):
        near = near + lax.ppermute(prior, "z", [(i, i + d) for i in range(planes - d)])
        near = near + lax.ppermute(prior, "z", [(i + d, i) for i in range(planes - d)])
    group = mem + ("y",)
    size = lax.axis_size(group)
    spread = lax.all_to_all(
        jnp.broadcast_to(near[None], (size, members, count)), group, 0, 0, tiled=True
    )
    spread = spread.reshape(size // rows_of_tiles, rows_of_tiles, members, count)

    state = lax.all_to_all(state, mem, 0, 0, tiled=True)
    state = state.reshape(-1, tile_rows, width)

    out = pl.pallas_call(
        analyse,
        out_shape=jax.ShapeDtypeStruct(state.shape, jnp.float32),
        in_specs=vmem_specs(5),
        out_specs=pl.BlockSpec(memory_space=pltpu.VMEM),
        compiler_params=params(),
        name="analyse",
    )(state, spread, fields, weight, cross)
    return out[:, None]


def solution(mesh):
    y = 4
    x = mesh.shape["mem"] // 2
    fine = Mesh(
        mesh.devices.reshape(x, 2, mesh.shape["space"] // y, y), ("x", "core", "z", "y")
    )
    mem, space = ("x", "core"), ("z", "y")
    placed = (P(mem, None, space, None), P(space, None), P(), P(), P(), P(), P(), P(), P())
    return jax.shard_map(
        shards, mesh=fine, in_specs=placed, out_specs=P(None, mem, space, None), check_vma=False
    )
```

time: 310 us -> 88.6 us (0.29)
  the two profiles are of different devices: /device:TPU:1 before, /device:TPU:385 now
where the time goes in v1:
time: 88.6 us; the launch traced here: 88 us
  blocking collectives  35.7 us (40%)
  starting transfers between devices  19.7 us (22%)
  Pallas kernels  14.2 us (16%)
  waiting for transfers between devices  9.77 us (11%)
  local copies, waits for them, and re-layouts  6.65 us (8%)
  other arithmetic  1.96 us (2%)
    all_to_all x1, blocking collectives, shards(): lax.all_to_all(jnp.broadcast_to(near[None], (size, members, count)), grou...  19.1 us
    all_to_all x1, blocking collectives, shards(): state = lax.all_to_all(state, mem, 0, 0, tiled=True)  16.5 us
    ppermute x2, starting transfers between devices, shards(): lax.ppermute(prior, 'z', [(i, i + d) for i in range(planes - d)])  6.9 us
    ppermute x1, waiting for transfers between devices, shards(): lax.ppermute(edges[:, tile_rows - HALO:], space, [(i, i + 1) for i in ran...  6.74 us
    unnamed x18, local copies, waits for them, and re-layouts  6.6 us
    pallas_call x1, Pallas kernels, shards(): pl.pallas_call(forecast, out_shape=[jax.ShapeDtypeStruct((levels, members...  6.36 us
    ppermute x1, starting transfers between devices, shards(): lax.ppermute(edges[:, :HALO], space, [(i + 1, i) for i in range(tiles - 1)])  6.3 us
    pallas_call x1, Pallas kernels, shards(): pl.pallas_call(analyse, out_shape=jax.ShapeDtypeStruct(state.shape, jnp.f...  6.03 us
  transfers between devices with their start and end apart: 6, of which 2 were waited for; matrix products, arithmetic and copies ran while one was open for 0% of the time, Pallas kernels for 2%

profile of v1, /device:TPU:385, one launch (start us, length us, event | category | flops | bytes accessed | tf_op | source)
XLA Modules:
  0.0 88.0 jit_solution(3985659493598518999)
XLA Ops:
  0.0 1.9 %pad_maximum_fusion = (f32[81,2,640]{2,1,0:T(2,128)S(1)}, f32[81,2,640]{2,1,0:T(2,128)S(1)}) fusion(f32[1,4,640]{2,1,0:T(4,128)} %bitcast.18, f32[80,4,640]{2,1,0:T(4,128)} %bitcast.16), kind=kLoop, calls=%fused_computation.3 | loop fusion | flops 207360 | bytes 1658880 | tf_op jit(solution)/shard_map/concatenate | solution.py:192
  1.9 6.3 %collective-permute-start.1 = (f32[81,2,640]{2,1,0:T(2,128)S(1)}, f32[81,2,640]{2,1,0:T(2,128)S(1)}, u32[]{:S(2)}, u32[]{:S(2)}) collective-permute-start(f32[81,2,640]{2,1,0:T(2,128)S(1)} %get-tuple-element.19), channel_id=1, source_target_pairs={{1,0},{2,1},{3,2},{4,3},{5,4},{6,5},{7,6},{8,7},{9,8},{10,9},{11,1... | collective-permute-start | bytes 1244168 | tf_op jit(solution)/shard_map/ppermute | solution.py:194
  8.2 1.9 %collective-permute-start = (f32[81,2,640]{2,1,0:T(2,128)S(1)}, f32[81,2,640]{2,1,0:T(2,128)S(1)}, u32[]{:S(2)}, u32[]{:S(2)}) collective-permute-start(f32[81,2,640]{2,1,0:T(2,128)S(1)} %get-tuple-element.20), channel_id=1, source_target_pairs={{0,1},{1,2},{2,3},{3,4},{4,5},{5,6},{6,7},{7,8},{8,9},{9,10},{10,1... | collective-permute-start | bytes 1244168 | tf_op jit(solution)/shard_map/ppermute | solution.py:193
  10.1 0.1 pad_add_fusion.refs_0_
  10.2 0.0 copy-start.2
  10.2 0.7 copy-done.2
  10.9 0.0 copy-start.3
  10.9 0.7 copy-done.3
  11.6 0.0 copy-start.4
  11.6 0.7 copy-done.4
  12.2 0.7 copy-done.5
  12.9 0.7 copy-done.6
  13.6 0.7 copy-done.7
  14.3 0.7 copy-done.8
  15.0 1.8 %prepare.1 = (f32[8,256]{1,0:T(8,128)S(1)}, f32[4,256,640]{2,1,0:T(8,128)S(1)}, f32[128,128]{1,0:T(8,128)S(1)}, bf16[640,256]{1,0:T(8,128)(2,1)S(1)}, f32[8,8,256]{2,1,0:T(8,128)S(1)}) custom-call(s32[2]{0:T(128)S(1)} %pad_add_fusion.refs_0_, s32[1,256]{1,0:T(1,128)S(1)} %bitcast.19, s32[1,256]{1,0:T(1,128)S(1)} %bitcast.20, s32[1,256]{1,0:T(1,128)S(1)} %bitcast.21, ...), custom_call_target="tpu_custom_call" | custom-call | flops 10000000 | bytes 4000000 | tf_op jit(solution)/shard_map/prepare/pallas_call | solution.py:197
  16.8 0.0 collective-permute-done.1.high_ref
  16.8 6.7 %collective-permute-done.low_ref = f32[81,2,640]{2,1,0:T(2,128)S(1)} collective-permute-done((f32[81,2,640]{2,1,0:T(2,128)S(1)}, f32[81,2,640]{2,1,0:T(2,128)S(1)}, u32[]{:S(2)}, u32[]{:S(2)}) %collective-permute-start) | collective-permute-done | bytes 414752 | tf_op jit(solution)/shard_map/ppermute | solution.py:193
  23.5 1.1 %copy-done = f32[10,8,4,640]{3,2,1,0:T(4,128)S(1)} copy-done((f32[10,8,4,640]{3,2,1,0:T(4,128)S(1)}, f32[10,8,4,640]{3,2,1,0:T(4,128)}, u32[]{:S(2)}) %copy-start) | copy-done | bytes 819224
  24.7 0.7 copy-done.1
  25.4 6.4 %forecast.1 = (f32[8,10,4,640]{3,2,1,0:T(4,128)S(1)}, f32[10,256]{1,0:T(8,128)S(1)}) custom-call(f32[10,8,4,640]{3,2,1,0:T(4,128)S(1)} %copy-done, f32[81,2,640]{2,1,0:T(2,128)S(1)} %collective-permute-done.low_ref, f32[81,2,640]{2,1,0:T(2,128)S(1)} %collective-permute-done.1.high_ref, f32[4,640]{1,0:T(4,128)S(1)} %copy-done.1, ...), custom_call_target="tpu_custom_call" | custom-call | tf_op jit(solution)/shard_map/forecast/pallas_call | solution.py:214
  31.7 1.9 %collective-permute-start.5 = (f32[10,256]{1,0:T(8,128)S(1)}, f32[10,256]{1,0:T(8,128)S(1)}, u32[]{:S(2)}, u32[]{:S(2)}) collective-permute-start(f32[10,256]{1,0:T(8,128)S(1)} %get-tuple-element.15), channel_id=1, source_target_pairs={{8,0},{12,4},{16,8},{20,12},{24,16},{28,20},{32,24},{36,28},{40,32... | collective-permute-start | bytes 30728 | tf_op jit(solution)/shard_map/ppermute | solution.py:234
  33.7 4.3 %collective-permute-start.4 = (f32[10,256]{1,0:T(8,128)S(1)}, f32[10,256]{1,0:T(8,128)S(1)}, u32[]{:S(2)}, u32[]{:S(2)}) collective-permute-start(f32[10,256]{1,0:T(8,128)S(1)} %get-tuple-element.15), channel_id=1, source_target_pairs={{0,8},{4,12},{8,16},{12,20},{16,24},{20,28},{24,32},{28,36},{32,40... | collective-permute-start | bytes 30728 | tf_op jit(solution)/shard_map/ppermute | solution.py:233
  37.9 2.6 %collective-permute-start.3 = (f32[10,256]{1,0:T(8,128)S(1)}, f32[10,256]{1,0:T(8,128)S(1)}, u32[]{:S(2)}, u32[]{:S(2)}) collective-permute-start(f32[10,256]{1,0:T(8,128)S(1)} %get-tuple-element.15), channel_id=1, source_target_pairs={{4,0},{8,4},{12,8},{16,12},{20,16},{24,20},{28,24},{32,28},{36,32}... | collective-permute-start | bytes 30728 | tf_op jit(solution)/shard_map/ppermute | solution.py:234
  40.6 2.6 %collective-permute-start.2 = (f32[10,256]{1,0:T(8,128)S(1)}, f32[10,256]{1,0:T(8,128)S(1)}, u32[]{:S(2)}, u32[]{:S(2)}) collective-permute-start(f32[10,256]{1,0:T(8,128)S(1)} %get-tuple-element.15), channel_id=1, source_target_pairs={{0,4},{4,8},{8,12},{12,16},{16,20},{20,24},{24,28},{28,32},{32,36}... | collective-permute-start | bytes 30728 | tf_op jit(solution)/shard_map/ppermute | solution.py:233
  43.2 0.0 collective-permute-done.5
  43.2 0.0 collective-permute-done.4
  43.2 0.0 collective-permute-done.3
  43.3 3.0 %collective-permute-done.2 = f32[10,256]{1,0:T(8,128)S(1)} collective-permute-done((f32[10,256]{1,0:T(8,128)S(1)}, f32[10,256]{1,0:T(8,128)S(1)}, u32[]{:S(2)}, u32[]{:S(2)}) %collective-permute-start.2) | collective-permute-done | bytes 10272 | tf_op jit(solution)/shard_map/ppermute | solution.py:233
  46.3 0.1 broadcast_in_dim.13
  46.3 19.1 %all_to_all.10 = f32[32,10,256]{2,1,0:T(8,128)S(1)} all-to-all(f32[32,10,256]{2,1,0:T(8,128)S(1)} %broadcast_in_dim.13), channel_id=1, replica_groups=mesh['x'=4,'core'=2,'z'=16,'y'=4] {'x','core','y'}, dimensions={0} | all-to-all | bytes 655360 | tf_op jit(solution)/shard_map/all_to_all | solution.py:237
  65.5 16.5 %all_to_all.11 = f32[8,10,4,640]{3,2,1,0:T(4,128)S(1)} all-to-all(f32[8,10,4,640]{3,2,1,0:T(4,128)S(1)} %get-tuple-element.14), channel_id=1, replica_groups=mesh['x'=4,'core'=2,'z'=16,'y'=4] {'x','core'}, dimensions={0} | all-to-all | bytes 1638400 | tf_op jit(solution)/shard_map/all_to_all | solution.py:242
  82.0 6.0 %analyse.1 = f32[80,4,640]{2,1,0:T(4,128)} custom-call(f32[80,4,640]{2,1,0:T(4,128)S(1)} %bitcast.15, f32[8,4,10,256]{3,2,1,0:T(8,128)S(1)} %bitcast.17, f32[8,256]{1,0:T(8,128)S(1)} %get-tuple-element.16.fields_ref, f32[4,256,640]{2,1,0:T(8,128)S(1)} %get-tuple-element.17.weight_ref, f32[128,128]{1,0:T(8,128)S(1)} %get-tuple-element.18.cross_ref), custom_call_target="tpu_custom_call" | custom-call | tf_op jit(solution)/shard_map/analyse/pallas_call | solution.py:245
  (7 shorter events, 0.0 us)
Async XLA Ops:
  1.9 14.9 %collective-permute-start.1 = (f32[81,2,640]{2,1,0:T(2,128)S(1)}, f32[81,2,640]{2,1,0:T(2,128)S(1)}, u32[]{:S(2)}, u32[]{:S(2)}) collective-permute-start(f32[81,2,640]{2,1,0:T(2,128)S(1)} %get-tuple-element.19), channel_id=1, source_target_pairs={{1,0},{2,1},{3,2},{4,3},{5,4},{6,5},{7,6},{8,7},{9,8},{10,9},{11,1... | collective-permute-start | bytes 1244168 | tf_op jit(solution)/shard_map/ppermute | solution.py:194
  8.2 15.3 %collective-permute-start = (f32[81,2,640]{2,1,0:T(2,128)S(1)}, f32[81,2,640]{2,1,0:T(2,128)S(1)}, u32[]{:S(2)}, u32[]{:S(2)}) collective-permute-start(f32[81,2,640]{2,1,0:T(2,128)S(1)} %get-tuple-element.20), channel_id=1, source_target_pairs={{0,1},{1,2},{2,3},{3,4},{4,5},{5,6},{6,7},{7,8},{8,9},{9,10},{10,1... | collective-permute-start | bytes 1244168 | tf_op jit(solution)/shard_map/ppermute | solution.py:193
  10.2 0.7 copy-start.2
  10.9 0.7 copy-start.3
  11.6 0.7 copy-start.4
  12.2 0.7 copy-start.5
  12.9 0.7 copy-start.6
  13.6 0.7 copy-start.7
  14.3 0.7 copy-start.8
  23.5 1.1 %copy-start = (f32[10,8,4,640]{3,2,1,0:T(4,128)S(1)}, f32[10,8,4,640]{3,2,1,0:T(4,128)}, u32[]{:S(2)}) copy-start(f32[10,8,4,640]{3,2,1,0:T(4,128)} %x_ref.1) | copy-start | bytes 2457604
  24.7 0.7 copy-start.1
  31.7 11.5 %collective-permute-start.5 = (f32[10,256]{1,0:T(8,128)S(1)}, f32[10,256]{1,0:T(8,128)S(1)}, u32[]{:S(2)}, u32[]{:S(2)}) collective-permute-start(f32[10,256]{1,0:T(8,128)S(1)} %get-tuple-element.15), channel_id=1, source_target_pairs={{8,0},{12,4},{16,8},{20,12},{24,16},{28,20},{32,24},{36,28},{40,32... | collective-permute-start | bytes 30728 | tf_op jit(solution)/shard_map/ppermute | solution.py:234
  33.7 9.6 %collective-permute-start.4 = (f32[10,256]{1,0:T(8,128)S(1)}, f32[10,256]{1,0:T(8,128)S(1)}, u32[]{:S(2)}, u32[]{:S(2)}) collective-permute-start(f32[10,256]{1,0:T(8,128)S(1)} %get-tuple-element.15), channel_id=1, source_target_pairs={{0,8},{4,12},{8,16},{12,20},{16,24},{20,28},{24,32},{28,36},{32,40... | collective-permute-start | bytes 30728 | tf_op jit(solution)/shard_map/ppermute | solution.py:233
  37.9 5.3 %collective-permute-start.3 = (f32[10,256]{1,0:T(8,128)S(1)}, f32[10,256]{1,0:T(8,128)S(1)}, u32[]{:S(2)}, u32[]{:S(2)}) collective-permute-start(f32[10,256]{1,0:T(8,128)S(1)} %get-tuple-element.15), channel_id=1, source_target_pairs={{4,0},{8,4},{12,8},{16,12},{20,16},{24,20},{28,24},{32,28},{36,32}... | collective-permute-start | bytes 30728 | tf_op jit(solution)/shard_map/ppermute | solution.py:234
  40.6 5.7 %collective-permute-start.2 = (f32[10,256]{1,0:T(8,128)S(1)}, f32[10,256]{1,0:T(8,128)S(1)}, u32[]{:S(2)}, u32[]{:S(2)}) collective-permute-start(f32[10,256]{1,0:T(8,128)S(1)} %get-tuple-element.15), channel_id=1, source_target_pairs={{0,4},{4,8},{8,12},{12,16},{16,20},{20,24},{24,28},{28,32},{32,36}... | collective-permute-start | bytes 30728 | tf_op jit(solution)/shard_map/ppermute | solution.py:233

commit v2 on v1

v2 whole, which is shorter than its diff:
```python
import jax
import jax.numpy as jnp
from jax import lax
from jax.experimental import pallas as pl
from jax.experimental.pallas import tpu as pltpu
from jax.sharding import Mesh
from jax.sharding import PartitionSpec as P

V = 4
OBS_BLOCK = 128
LOC_RADIUS = 16
ADVECT = 0.15
HALO = 2
LANES = 128
FULL = lax.Precision.HIGHEST


def vmem_specs(count):
    return [pl.BlockSpec(memory_space=pltpu.VMEM)] * count


def hbm_specs(count):
    return [pl.BlockSpec(memory_space=pltpu.HBM)] * count


def in_hbm(*arrays):
    return [pltpu.with_memory_space_constraint(a, pltpu.HBM) for a in arrays]


def fetch(pairs, sems):
    copies = [pltpu.make_async_copy(a, b, sems.at[i]) for i, (a, b) in enumerate(pairs)]
    for copy in copies:
        copy.start()
    for copy in copies:
        copy.wait()


def params(mib):
    return pltpu.CompilerParams(vmem_limit_bytes=mib * 1024 * 1024)


def prepare(tile_rows, width, place_ref, row_hbm, lon_hbm, lev_hbm, order_hbm, value_hbm, error_hbm,
            coupling_hbm, fields_ref, weight_ref, cross_ref, onehot_ref, pick_ref,
            ints, floats, coupling_ref, sems):
    count = row_hbm.shape[1]
    fetch(
        [(ref, ints.at[i]) for i, ref in enumerate((row_hbm, lon_hbm, lev_hbm, order_hbm))]
        + [(ref, floats.at[i]) for i, ref in enumerate((value_hbm, error_hbm))]
        + [(coupling_hbm, coupling_ref)],
        sems,
    )
    levels = coupling_ref.shape[0]
    tile_start = place_ref[0]
    own_level = place_ref[1]
    fields = jnp.concatenate(
        [
            ints[0].astype(jnp.float32),
            ints[1].astype(jnp.float32),
            ints[2].astype(jnp.float32),
            floats[0],
            floats[1],
            jnp.zeros((3, count), jnp.float32),
        ],
        axis=0,
    )
    source = lax.broadcasted_iota(jnp.int32, (count, count), 0)
    taken = (source == ints[3]).astype(jnp.float32)
    ordered = jnp.dot(fields, taken, precision=FULL, preferred_element_type=jnp.float32)
    fields_ref[...] = ordered
    rows = ordered[0:1]
    lons = ordered[1:2]
    levs = ordered[2:3]
    columns = jnp.concatenate([ordered, jnp.zeros((LANES - 8, count), jnp.float32)], axis=0).T
    row_col = columns[:, 0:1]
    lon_col = columns[:, 1:2]
    lev_col = columns[:, 2:3]

    def near(drow, dlon):
        dlon = jnp.minimum(dlon, width - dlon)
        close = jnp.maximum(0.0, 1.0 - (drow + dlon) / LOC_RADIUS)
        return close * close

    coupled = jnp.zeros((count, levels), jnp.float32)
    coupled_own = jnp.zeros((count, 1), jnp.float32)
    table = coupling_ref[...]
    lane = lax.broadcasted_iota(jnp.int32, (levels, levels), 1)
    own = jnp.sum(jnp.where(lane == own_level, table, 0.0), axis=1, keepdims=True)
    for level in range(levels):
        here = lev_col == level
        coupled = jnp.where(here, table[level:level + 1, :], coupled)
        coupled_own = jnp.where(here, own[level:level + 1, :], coupled_own)
    cell_lon = lax.broadcasted_iota(jnp.int32, (1, width), 1).astype(jnp.float32)
    dlon = jnp.abs(cell_lon - lon_col)
    for row in range(tile_rows):
        drow = jnp.abs((tile_start + row).astype(jnp.float32) - row_col)
        weight_ref[:, row * width:(row + 1) * width] = coupled_own * near(drow, dlon)

    first = slice(0, OBS_BLOCK)
    second = slice(OBS_BLOCK, 2 * OBS_BLOCK)
    between = jnp.zeros((OBS_BLOCK, OBS_BLOCK), jnp.float32)
    for level in range(levels):
        between = jnp.where(levs[:, second] == level, coupled[first, level:level + 1], between)
    cross_ref[...] = between * near(
        jnp.abs(row_col[first] - rows[:, second]), jnp.abs(lon_col[first] - lons[:, second])
    )

    lon_id = lax.broadcasted_iota(jnp.int32, (width, count), 0).astype(jnp.float32)
    onehot_ref[...] = (lon_id == lons).astype(jnp.bfloat16)
    heights = levels // V
    slot = lax.broadcasted_iota(jnp.int32, (8, count), 0)
    height = slot // tile_rows
    inside = rows - tile_start.astype(jnp.float32) == (slot - height * tile_rows).astype(jnp.float32)
    for v in range(V):
        there = levs == (v * heights + height).astype(jnp.float32)
        pick_ref[v] = jnp.where(inside & there, 1.0, 0.0)


def edges(x_hbm, diff_hbm, up_ref, down_ref, held_ref, diff_ref, sems):
    tile_rows = x_hbm.shape[1]
    extra = x_hbm.shape[0]
    fetch([(x_hbm, held_ref), (diff_hbm, diff_ref)], sems)
    up_ref[0:extra] = held_ref[:, tile_rows - HALO:, :]
    down_ref[0:extra] = held_ref[:, :HALO, :]
    up_ref[extra] = diff_ref[tile_rows - HALO:, :]
    down_ref[extra] = diff_ref[:HALO, :]


def forecast(x_hbm, diff_hbm, low_hbm, high_hbm, onehot_ref, pick_ref, prior_ref, out_hbm,
             wide_ref, own_ref, pair_ref, diff_ref, diff_sems, in_sems, out_sems):
    members, levels, tile_rows, width = x_hbm.shape
    heights = levels // V
    deep = tile_rows + 2 * HALO
    extra = members * levels
    top, own, bottom = pl.ds(0, HALO), pl.ds(HALO, tile_rows), pl.ds(HALO + tile_rows, HALO)

    def arrivals(member):
        part = pl.ds(member * levels, levels)
        return [
            pltpu.make_async_copy(x_hbm.at[member], wide_ref.at[member, :, own], in_sems.at[member, 0]),
            pltpu.make_async_copy(low_hbm.at[part], wide_ref.at[member, :, top], in_sems.at[member, 1]),
            pltpu.make_async_copy(high_hbm.at[part], wide_ref.at[member, :, bottom], in_sems.at[member, 2]),
        ]

    def departure(member):
        return pltpu.make_async_copy(own_ref.at[:, member], out_hbm.at[:, member], out_sems.at[member])

    diffs = [
        pltpu.make_async_copy(diff_hbm, diff_ref.at[own], diff_sems.at[0]),
        pltpu.make_async_copy(low_hbm.at[extra], diff_ref.at[top], diff_sems.at[1]),
        pltpu.make_async_copy(high_hbm.at[extra], diff_ref.at[bottom], diff_sems.at[2]),
    ]
    for copy in diffs:
        copy.start()
    for member in range(members):
        for copy in arrivals(member):
            copy.start()
    for copy in diffs:
        copy.wait()
    diff = diff_ref[...]
    keep = 1.0 - 4.0 * diff
    upper = lax.broadcasted_iota(jnp.int32, (deep, width), 0) < tile_rows

    def sub_step(fields):
        push_u, push_w = ADVECT * fields[0], ADVECT * fields[1]
        from_east, from_west = diff - push_u, diff + push_u
        from_north, from_south = diff - push_w, diff + push_w
        return [
            keep * q
            + (from_east * pltpu.roll(q, width - 1, 1) + from_west * pltpu.roll(q, 1, 1))
            + (from_north * pltpu.roll(q, deep - 1, 0) + from_south * pltpu.roll(q, 1, 0))
            for q in fields
        ]

    @pl.loop(0, members)
    def _(member):
        for copy in arrivals(member):
            copy.wait()
        done = []
        for height in range(heights):
            fields = sub_step(sub_step([wide_ref[member, v * heights + height] for v in range(V)]))
            for v in range(V):
                own_ref[v * heights + height, member] = fields[v][HALO:HALO + tile_rows]
            done.append(fields)
        departure(member).start()
        for v in range(V):
            pair_ref[v, member] = jnp.where(
                upper, pltpu.roll(done[0][v], deep - HALO, 0), pltpu.roll(done[1][v], HALO, 0)
            )

    count = onehot_ref.shape[1]
    total = jnp.zeros((members, deep, count), jnp.float32)
    for v in range(V):
        rest = pair_ref[v].reshape(members * deep, width)
        found = jnp.zeros((members * deep, count), jnp.float32)
        for _ in range(3):
            part = rest.astype(jnp.bfloat16)
            rest = rest - part.astype(jnp.float32)
            found = found + jnp.dot(part, onehot_ref[...], preferred_element_type=jnp.float32)
        total = total + found.reshape(members, deep, -1) * pick_ref[v][None]
    prior = jnp.sum(total, axis=1)
    for m in range(members):
        prior_ref[:, m * count:(m + 1) * count] = prior[m:m + 1]
    for member in range(members):
        departure(member).wait()


def split(a):
    high = a.astype(jnp.bfloat16)
    return high, (a - high.astype(jnp.float32)).astype(jnp.bfloat16)

def exactdot(a, b):
    return jnp.dot(a, b, precision=lax.Precision.HIGHEST, preferred_element_type=jnp.float32)

def adjust(prior, values, errors):
    members = prior.shape[0]
    mean = jnp.sum(prior, axis=0, keepdims=True) / members
    dev = prior - mean
    var = jnp.sum(dev * dev, axis=0, keepdims=True) / (members - 1) + 1e-06
    post_var = 1.0 / (1.0 / var + 1.0 / errors)
    post_mean = post_var * (mean / var + values / errors)
    shrink = jnp.sqrt(errors / (errors + var))
    incr = post_mean + shrink * dev - prior
    gain = dev / ((members - 1) * var)
    return incr, gain

def three(a, axis):
    high, low = split(a)
    order = [high, high, low] if axis == 1 else [high, low, high]
    return jnp.concatenate(order, axis=axis)

def thin(gain):
    high = gain.astype(jnp.bfloat16).astype(jnp.float32)
    return jnp.concatenate([high, high, gain - high], axis=0).T.astype(jnp.bfloat16)

def onedot(a, b):
    return jnp.dot(a, b, preferred_element_type=jnp.float32)

def analyse(x_ref, prior_ref, fields_ref, weight_ref, cross_ref, out_ref, scratch):
    members, tile_rows, width = x_ref.shape
    planes, tiles, _, _ = prior_ref.shape
    count = fields_ref.shape[1]
    share = members // planes
    for i in range(planes):
        for m in range(share):
            at = slice(m * count, (m + 1) * count)
            line = prior_ref[i, 0, :, at]
            for t in range(1, tiles):
                line = line + prior_ref[i, t, :, at]
            scratch[i * share + m:i * share + m + 1, :] = line
    prior = scratch[...]
    values = fields_ref[3:4]
    errors = fields_ref[4:5]
    first = slice(0, OBS_BLOCK)
    second = slice(OBS_BLOCK, 2 * OBS_BLOCK)
    incr0, gain0 = adjust(prior[:, first], values[:, first], errors[:, first])
    later = prior[:, second]
    later = later + exactdot(incr0, cross_ref[...] * exactdot(gain0.T, later))
    incr1, gain1 = adjust(later, values[:, second], errors[:, second])
    incr0, incr1 = three(incr0, 1), three(incr1, 1)
    gain0, gain1 = thin(gain0), thin(gain1)
    x = jnp.concatenate([x_ref[:, row, :] for row in range(tile_rows)], axis=1)
    x = x + onedot(incr0, three(weight_ref[first, :] * onedot(gain0, three(x, 0)), 0))
    x = x + onedot(incr1, three(weight_ref[second, :] * onedot(gain1, three(x, 0)), 0))
    for row in range(tile_rows):
        out_ref[:, row, :] = x[:, row * width:(row + 1) * width]


def shards(ensemble, diffusivity, obs_row, obs_lon, obs_level, obs_order, obs_value, obs_error, coupling):
    members, levels, tile_rows, width = ensemble.shape
    count = obs_row.shape[0]
    space = ("z", "y")
    mem = ("x", "core")
    tiles = lax.axis_size(space)
    planes = lax.axis_size("z")
    own_level = lax.axis_index(mem)
    place = jnp.stack([lax.axis_index(space) * tile_rows, own_level]).astype(jnp.int32)
    cells = tile_rows * width
    shape = jax.ShapeDtypeStruct
    f32 = jnp.float32

    extra = members * levels
    flat = ensemble.reshape(extra, tile_rows, width)
    up, down = pl.pallas_call(
        edges,
        out_shape=[
            shape((extra + 1, HALO, width), f32),
            shape((extra + 1, HALO, width), f32),
        ],
        in_specs=hbm_specs(2),
        out_specs=vmem_specs(2),
        scratch_shapes=[
            pltpu.VMEM((extra, tile_rows, width), f32),
            pltpu.VMEM((tile_rows, width), f32),
            pltpu.SemaphoreType.DMA((2,)),
        ],
        compiler_params=params(8),
        name="edges",
    )(*in_hbm(flat, diffusivity))
    low = lax.ppermute(up, space, [(i, i + 1) for i in range(tiles - 1)])
    high = lax.ppermute(down, space, [(i + 1, i) for i in range(tiles - 1)])

    line = lambda a: a.reshape(1, count)
    fields, weight, cross, onehot, pick = pl.pallas_call(
        lambda *refs: prepare(tile_rows, width, *refs),
        out_shape=[
            shape((8, count), f32),
            shape((count, cells), f32),
            shape((OBS_BLOCK, OBS_BLOCK), f32),
            shape((width, count), jnp.bfloat16),
            shape((V, 8, count), f32),
        ],
        in_specs=[pl.BlockSpec(memory_space=pltpu.SMEM)] + hbm_specs(7),
        out_specs=vmem_specs(5),
        scratch_shapes=[
            pltpu.VMEM((4, 1, count), jnp.int32),
            pltpu.VMEM((2, 1, count), f32),
            pltpu.VMEM((levels, levels), f32),
            pltpu.SemaphoreType.DMA((7,)),
        ],
        compiler_params=params(16),
        cost_estimate=pl.CostEstimate(flops=10_000_000, bytes_accessed=4_000_000, transcendentals=0),
        name="prepare",
    )(place, *in_hbm(line(obs_row), line(obs_lon), line(obs_level), line(obs_order), line(obs_value),
                     line(obs_error), coupling))

    deep = tile_rows + 2 * HALO
    prior, state = pl.pallas_call(
        forecast,
        out_shape=[
            shape((1, members * count), f32),
            pltpu.HBM((levels, members, tile_rows, width), f32),
        ],
        in_specs=hbm_specs(4) + vmem_specs(2),
        out_specs=vmem_specs(1) + hbm_specs(1),
        scratch_shapes=[
            pltpu.VMEM((members, levels, deep, width), f32),
            pltpu.VMEM((levels, members, tile_rows, width), f32),
            pltpu.VMEM((V, members, deep, width), f32),
            pltpu.VMEM((deep, width), f32),
            pltpu.SemaphoreType.DMA((3,)),
            pltpu.SemaphoreType.DMA((members, 3)),
            pltpu.SemaphoreType.DMA((members,)),
        ],
        compiler_params=params(16),
        name="forecast",
    )(*in_hbm(ensemble, diffusivity), low, high, onehot, pick)

    reach = 2 * (LOC_RADIUS - 1)
    tiles_reached = -(-reach // tile_rows)
    rows_of_tiles = tiles // planes
    planes_reached = min(-(-tiles_reached // rows_of_tiles), planes - 1)
    near = prior
    for d in range(1, planes_reached + 1):
        near = near + lax.ppermute(prior, "z", [(i, i + d) for i in range(planes - d)])
        near = near + lax.ppermute(prior, "z", [(i + d, i) for i in range(planes - d)])
    state = lax.all_to_all(state, mem, 0, 0, tiled=True)
    near, state = lax.optimization_barrier((near, state))
    group = mem + ("y",)
    size = lax.axis_size(group)
    spread = lax.all_to_all(
        jnp.broadcast_to(near[None], (size,) + near.shape), group, 0, 0, tiled=True
    )
    spread = spread.reshape((size // rows_of_tiles, rows_of_tiles) + near.shape)
    state = state.reshape(-1, tile_rows, width)

    out = pl.pallas_call(
        analyse,
        out_shape=shape(state.shape, f32),
        in_specs=vmem_specs(5),
        out_specs=pl.BlockSpec(memory_space=pltpu.VMEM),
        scratch_shapes=[pltpu.VMEM((state.shape[0], count), f32)],
        compiler_params=params(24),
        name="analyse",
    )(state, spread, fields, weight, cross)
    return out[:, None]


def solution(mesh):
    y = 4
    x = mesh.shape["mem"] // 2
    fine = Mesh(
        mesh.devices.reshape(x, 2, mesh.shape["space"] // y, y), ("x", "core", "z", "y")
    )
    mem, space = ("x", "core"), ("z", "y")
    placed = (P(mem, None, space, None), P(space, None), P(), P(), P(), P(), P(), P(), P())
    return jax.shard_map(
        shards, mesh=fine, in_specs=placed, out_specs=P(None, mem, space, None), check_vma=False
    )
```

time: 88.6 us -> 70.9 us (0.80)
  blocking collectives: 35.7 us -> 21 us
  starting transfers between devices: 19.7 us -> 26.7 us
  local copies, waits for them, and re-layouts: 6.65 us -> 0.17 us
  other arithmetic: 1.96 us -> 0.13 us
  Pallas kernels: 14.2 us -> 13.1 us
    all_to_all x2 -> x1, blocking collectives: 35.7 us -> 21 us  [shards(): lax.all_to_all(jnp.broadcast_to(near[None], (size,) + near.shape), group,...]
    unnamed x18 -> x0, local copies, waits for them, and re-layouts: 6.6 us -> none
    all_to_all x0 -> x1, starting transfers between devices: none -> 6.17 us  [shards(): state = lax.all_to_all(state, mem, 0, 0, tiled=True)]
    ppermute x2, starting transfers between devices: 4.57 us -> 6.92 us  [shards(): lax.ppermute(prior, 'z', [(i + d, i) for i in range(planes - d)])]
    pallas_call x2 -> x3, Pallas kernels: 12.4 us -> 10.5 us  [the longest x1 5.47 us: shards(): pl.pallas_call(forecast, out_shape=[shape((1, members * count), f32), plt...]
    ppermute x2, starting transfers between devices: 6.9 us -> 5.02 us  [shards(): lax.ppermute(prior, 'z', [(i, i + d) for i in range(planes - d)])]
    concatenate x1 -> x0, other arithmetic: 1.87 us -> none  [shards(): edges = jnp.concatenate([flat, diffusivity[None]], axis=0)]
    ppermute x2, waiting for transfers between devices: 6.74 us -> 5.49 us  [the longest x1 4.52 us: shards(): low = lax.ppermute(up, space, [(i, i + 1) for i in range(tiles - 1)])]
  transfers between devices with their start and end apart: 6 -> 7, of which waited for: 2 -> 3; matrix products, arithmetic and copies ran while one was open for 0% -> 0% of each run, Pallas kernels for 2% -> 4%
where the time goes in v2:
time: 70.9 us; the launch traced here: 70.5 us
  starting transfers between devices  26.7 us (38%)
  blocking collectives  21 us (30%)
  Pallas kernels  13.1 us (18%)
  waiting for transfers between devices  9.17 us (13%)
    all_to_all x1, blocking collectives, shards(): lax.all_to_all(jnp.broadcast_to(near[None], (size,) + near.shape), group,...  21 us
    ppermute x2, starting transfers between devices, shards(): lax.ppermute(prior, 'z', [(i + d, i) for i in range(planes - d)])  6.92 us
    all_to_all x1, starting transfers between devices, shards(): state = lax.all_to_all(state, mem, 0, 0, tiled=True)  6.17 us
    pallas_call x1, Pallas kernels, shards(): pl.pallas_call(forecast, out_shape=[shape((1, members * count), f32), plt...  5.47 us
    ppermute x1, starting transfers between devices, shards(): high = lax.ppermute(down, space, [(i + 1, i) for i in range(tiles - 1)])  5.4 us
    ppermute x2, starting transfers between devices, shards(): lax.ppermute(prior, 'z', [(i, i + d) for i in range(planes - d)])  5.02 us
    ppermute x1, waiting for transfers between devices, shards(): low = lax.ppermute(up, space, [(i, i + 1) for i in range(tiles - 1)])  4.52 us
    ppermute x2, waiting for transfers between devices, shards(): lax.ppermute(prior, 'z', [(i, i + d) for i in range(planes - d)])  3.67 us
  transfers between devices with their start and end apart: 7, of which 3 were waited for; matrix products, arithmetic and copies ran while one was open for 0% of the time, Pallas kernels for 4%

profile of v2, /device:TPU:385, one launch (start us, length us, event | category | flops | bytes accessed | tf_op | source)
XLA Modules:
  0.0 70.5 jit_solution(17318242525113544730)
XLA Ops:
  0.0 2.3 %edges.1 = (f32[81,2,640]{2,1,0:T(2,128)}, f32[81,2,640]{2,1,0:T(2,128)}) custom-call(f32[80,4,640]{2,1,0:T(4,128)} %bitcast.16, f32[4,640]{1,0:T(4,128)} %diff_hbm.3), custom_call_target="tpu_custom_call" | custom-call | tf_op jit(solution)/shard_map/edges/pallas_call | solution.py:283
  2.3 3.2 %collective-permute-start = (f32[81,2,640]{2,1,0:T(2,128)}, f32[81,2,640]{2,1,0:T(2,128)S(1)}, u32[]{:S(2)}, u32[]{:S(2)}) collective-permute-start(f32[81,2,640]{2,1,0:T(2,128)} %get-tuple-element.16), channel_id=1, source_target_pairs={{0,1},{1,2},{2,3},{3,4},{4,5},{5,6},{6,7},{7,8},{8,9},{9,10},{10,1... | collective-permute-start | bytes 1244168 | tf_op jit(solution)/shard_map/ppermute | solution.py:299
  5.5 5.4 %collective-permute-start.1 = (f32[81,2,640]{2,1,0:T(2,128)}, f32[81,2,640]{2,1,0:T(2,128)}, u32[]{:S(2)}, u32[]{:S(2)}) collective-permute-start(f32[81,2,640]{2,1,0:T(2,128)} %get-tuple-element.17), channel_id=1, source_target_pairs={{1,0},{2,1},{3,2},{4,3},{5,4},{6,5},{7,6},{8,7},{9,8},{10,9},{11,1... | collective-permute-start | bytes 1244168 | tf_op jit(solution)/shard_map/ppermute | solution.py:300
  10.9 0.1 pad_add_fusion.refs_0_
  11.0 2.6 %prepare.1 = (f32[8,256]{1,0:T(8,128)S(1)}, f32[256,2560]{1,0:T(8,128)S(1)}, f32[128,128]{1,0:T(8,128)S(1)}, bf16[640,256]{1,0:T(8,128)(2,1)S(1)}, f32[4,8,256]{2,1,0:T(8,128)S(1)}) custom-call(s32[2]{0:T(128)S(1)} %pad_add_fusion.refs_0_, s32[1,256]{1,0:T(1,128)} %bitcast.17, s32[1,256]{1,0:T(1,128)} %bitcast.18, s32[1,256]{1,0:T(1,128)} %bitcast.19, ...), custom_call_target="tpu_custom_call" | custom-call | flops 10000000 | bytes 4000000 | tf_op jit(solution)/shard_map/prepare/pallas_call | solution.py:303
  13.7 4.5 %collective-permute-done.low_hbm = f32[81,2,640]{2,1,0:T(2,128)S(1)} collective-permute-done((f32[81,2,640]{2,1,0:T(2,128)}, f32[81,2,640]{2,1,0:T(2,128)S(1)}, u32[]{:S(2)}, u32[]{:S(2)}) %collective-permute-start) | collective-permute-done | bytes 414752 | tf_op jit(solution)/shard_map/ppermute | solution.py:299
  18.2 1.0 %collective-permute-done.1.high_hbm = f32[81,2,640]{2,1,0:T(2,128)} collective-permute-done((f32[81,2,640]{2,1,0:T(2,128)}, f32[81,2,640]{2,1,0:T(2,128)}, u32[]{:S(2)}, u32[]{:S(2)}) %collective-permute-start.1) | collective-permute-done | bytes 414752 | tf_op jit(solution)/shard_map/ppermute | solution.py:300
  19.1 5.5 %forecast.1 = (f32[1,2560]{1,0:T(1,128)S(1)}, f32[8,10,4,640]{3,2,1,0:T(4,128)}) custom-call(f32[10,8,4,640]{3,2,1,0:T(4,128)} %x_hbm.1, f32[4,640]{1,0:T(4,128)} %diff_hbm.3, f32[81,2,640]{2,1,0:T(2,128)S(1)} %collective-permute-done.low_hbm, f32[81,2,640]{2,1,0:T(2,128)} %collective-permute-done.1.high_hbm, ...), custom_call_target="tpu_custom_call" | custom-call | tf_op jit(solution)/shard_map/forecast/pallas_call | solution.py:327
  24.6 6.2 %all-to-all-start = ((f32[8,10,4,640]{3,2,1,0:T(4,128)}), f32[8,10,4,640]{3,2,1,0:T(4,128)S(1)}, u32[]{:S(2)}, u32[]{:S(2)}) async-start(f32[8,10,4,640]{3,2,1,0:T(4,128)} %get-tuple-element.21), calls=%async_computation | async-start | bytes 1638400 | tf_op jit(solution)/shard_map/all_to_all | solution.py:356
  30.8 3.1 %collective-permute-start.5 = (f32[1,2560]{1,0:T(1,128)S(1)}, f32[1,2560]{1,0:T(1,128)S(1)}, u32[]{:S(2)}, u32[]{:S(2)}) collective-permute-start(f32[1,2560]{1,0:T(1,128)S(1)} %get-tuple-element.20), channel_id=1, source_target_pairs={{8,0},{12,4},{16,8},{20,12},{24,16},{28,20},{32,24},{36,28},{40,32... | collective-permute-start | bytes 30728 | tf_op jit(solution)/shard_map/ppermute | solution.py:355
  33.9 3.1 %collective-permute-start.4 = (f32[1,2560]{1,0:T(1,128)S(1)}, f32[1,2560]{1,0:T(1,128)S(1)}, u32[]{:S(2)}, u32[]{:S(2)}) collective-permute-start(f32[1,2560]{1,0:T(1,128)S(1)} %get-tuple-element.20), channel_id=1, source_target_pairs={{0,8},{4,12},{8,16},{12,20},{16,24},{20,28},{24,32},{28,36},{32,40... | collective-permute-start | bytes 30728 | tf_op jit(solution)/shard_map/ppermute | solution.py:354
  37.0 3.9 %collective-permute-start.3 = (f32[1,2560]{1,0:T(1,128)S(1)}, f32[1,2560]{1,0:T(1,128)S(1)}, u32[]{:S(2)}, u32[]{:S(2)}) collective-permute-start(f32[1,2560]{1,0:T(1,128)S(1)} %get-tuple-element.20), channel_id=1, source_target_pairs={{4,0},{8,4},{12,8},{16,12},{20,16},{24,20},{28,24},{32,28},{36,32}... | collective-permute-start | bytes 30728 | tf_op jit(solution)/shard_map/ppermute | solution.py:355
  40.8 1.9 %collective-permute-start.2 = (f32[1,2560]{1,0:T(1,128)S(1)}, f32[1,2560]{1,0:T(1,128)S(1)}, u32[]{:S(2)}, u32[]{:S(2)}) collective-permute-start(f32[1,2560]{1,0:T(1,128)S(1)} %get-tuple-element.20), channel_id=1, source_target_pairs={{0,4},{4,8},{8,12},{12,16},{16,20},{20,24},{24,28},{28,32},{32,36}... | collective-permute-start | bytes 30728 | tf_op jit(solution)/shard_map/ppermute | solution.py:354
  42.8 0.0 collective-permute-done.5
  42.8 0.0 collective-permute-done.4
  42.8 0.0 collective-permute-done.3
  42.8 3.7 %collective-permute-done.2 = f32[1,2560]{1,0:T(1,128)S(1)} collective-permute-done((f32[1,2560]{1,0:T(1,128)S(1)}, f32[1,2560]{1,0:T(1,128)S(1)}, u32[]{:S(2)}, u32[]{:S(2)}) %collective-permute-start.2) | collective-permute-done | bytes 10272 | tf_op jit(solution)/shard_map/ppermute | solution.py:354
  46.5 0.0 all-to-all-done
  46.5 0.2 broadcast_in_dim.12
  46.7 21.0 %all_to_all.10 = f32[32,1,2560]{2,1,0:T(1,128)S(1)} all-to-all(f32[32,1,2560]{2,1,0:T(1,128)S(1)} %broadcast_in_dim.12), channel_id=1, replica_groups=mesh['x'=4,'core'=2,'z'=16,'y'=4] {'x','core','y'}, dimensions={0} | all-to-all | bytes 655360 | tf_op jit(solution)/shard_map/all_to_all | solution.py:360
  67.7 2.7 %analyse.1 = f32[80,4,640]{2,1,0:T(4,128)} custom-call(f32[80,4,640]{2,1,0:T(4,128)S(1)} %bitcast.14, f32[8,4,1,2560]{3,2,1,0:T(1,128)S(1)} %bitcast.15, f32[8,256]{1,0:T(8,128)S(1)} %get-tuple-element.24.fields_ref, f32[256,2560]{1,0:T(8,128)S(1)} %get-tuple-element.25.weight_ref, f32[128,128]{1,0:T(8,128)S(1)} %get-tuple-element.26.cross_ref), custom_call_target="tpu_custom_call" | custom-call | tf_op jit(solution)/shard_map/analyse/pallas_call | solution.py:366
  (2 shorter events, 0.1 us)
Async XLA Ops:
  2.3 15.9 %collective-permute-start = (f32[81,2,640]{2,1,0:T(2,128)}, f32[81,2,640]{2,1,0:T(2,128)S(1)}, u32[]{:S(2)}, u32[]{:S(2)}) collective-permute-start(f32[81,2,640]{2,1,0:T(2,128)} %get-tuple-element.16), channel_id=1, source_target_pairs={{0,1},{1,2},{2,3},{3,4},{4,5},{5,6},{6,7},{7,8},{8,9},{9,10},{10,1... | collective-permute-start | bytes 1244168 | tf_op jit(solution)/shard_map/ppermute | solution.py:299
  5.5 13.6 %collective-permute-start.1 = (f32[81,2,640]{2,1,0:T(2,128)}, f32[81,2,640]{2,1,0:T(2,128)}, u32[]{:S(2)}, u32[]{:S(2)}) collective-permute-start(f32[81,2,640]{2,1,0:T(2,128)} %get-tuple-element.17), channel_id=1, source_target_pairs={{1,0},{2,1},{3,2},{4,3},{5,4},{6,5},{7,6},{8,7},{9,8},{10,9},{11,1... | collective-permute-start | bytes 1244168 | tf_op jit(solution)/shard_map/ppermute | solution.py:300
  24.6 21.9 %all-to-all-start = ((f32[8,10,4,640]{3,2,1,0:T(4,128)}), f32[8,10,4,640]{3,2,1,0:T(4,128)S(1)}, u32[]{:S(2)}, u32[]{:S(2)}) async-start(f32[8,10,4,640]{3,2,1,0:T(4,128)} %get-tuple-element.21), calls=%async_computation | async-start | bytes 1638400 | tf_op jit(solution)/shard_map/all_to_all | solution.py:356
  30.8 12.0 %collective-permute-start.5 = (f32[1,2560]{1,0:T(1,128)S(1)}, f32[1,2560]{1,0:T(1,128)S(1)}, u32[]{:S(2)}, u32[]{:S(2)}) collective-permute-start(f32[1,2560]{1,0:T(1,128)S(1)} %get-tuple-element.20), channel_id=1, source_target_pairs={{8,0},{12,4},{16,8},{20,12},{24,16},{28,20},{32,24},{36,28},{40,32... | collective-permute-start | bytes 30728 | tf_op jit(solution)/shard_map/ppermute | solution.py:355
  33.9 8.9 %collective-permute-start.4 = (f32[1,2560]{1,0:T(1,128)S(1)}, f32[1,2560]{1,0:T(1,128)S(1)}, u32[]{:S(2)}, u32[]{:S(2)}) collective-permute-start(f32[1,2560]{1,0:T(1,128)S(1)} %get-tuple-element.20), channel_id=1, source_target_pairs={{0,8},{4,12},{8,16},{12,20},{16,24},{20,28},{24,32},{28,36},{32,40... | collective-permute-start | bytes 30728 | tf_op jit(solution)/shard_map/ppermute | solution.py:354
  37.0 5.8 %collective-permute-start.3 = (f32[1,2560]{1,0:T(1,128)S(1)}, f32[1,2560]{1,0:T(1,128)S(1)}, u32[]{:S(2)}, u32[]{:S(2)}) collective-permute-start(f32[1,2560]{1,0:T(1,128)S(1)} %get-tuple-element.20), channel_id=1, source_target_pairs={{4,0},{8,4},{12,8},{16,12},{20,16},{24,20},{28,24},{32,28},{36,32}... | collective-permute-start | bytes 30728 | tf_op jit(solution)/shard_map/ppermute | solution.py:355
  40.8 5.6 %collective-permute-start.2 = (f32[1,2560]{1,0:T(1,128)S(1)}, f32[1,2560]{1,0:T(1,128)S(1)}, u32[]{:S(2)}, u32[]{:S(2)}) collective-permute-start(f32[1,2560]{1,0:T(1,128)S(1)} %get-tuple-element.20), channel_id=1, source_target_pairs={{0,4},{4,8},{8,12},{12,16},{16,20},{20,24},{24,28},{28,32},{32,36}... | collective-permute-start | bytes 30728 | tf_op jit(solution)/shard_map/ppermute | solution.py:354

commit v3 on v2

--- a/solution.py
+++ b/solution.py
@@ -115,17 +115,35 @@
         pick_ref[v] = jnp.where(inside & there, 1.0, 0.0)
 
 
-def edges(x_hbm, diff_hbm, up_ref, down_ref, held_ref, diff_ref, sems):
-    tile_rows = x_hbm.shape[1]
-    extra = x_hbm.shape[0]
-    fetch([(x_hbm, held_ref), (diff_hbm, diff_ref)], sems)
-    up_ref[0:extra] = held_ref[:, tile_rows - HALO:, :]
-    down_ref[0:extra] = held_ref[:, :HALO, :]
-    up_ref[extra] = diff_ref[tile_rows - HALO:, :]
-    down_ref[extra] = diff_ref[:HALO, :]
-
-
-def forecast(x_hbm, diff_hbm, low_hbm, high_hbm, onehot_ref, pick_ref, prior_ref, out_hbm,
+def edges(place_ref, x_hbm, diff_hbm, first_ref, second_ref, held_ref, diff_ref, sems):
+    members, levels, tile_rows, width = x_hbm.shape
+    extra = members * levels
+    odd = place_ref[2] == 1
+    copies = [pltpu.make_async_copy(diff_hbm, diff_ref, sems.at[members])]
+    copies += [pltpu.make_async_copy(x_hbm.at[i], held_ref.at[i], sems.at[i]) for i in range(members)]
+    for copy in copies:
+        copy.start()
+
+    def give(low_ref, high_ref):
+        for member in range(members):
+            part = slice(member * levels, (member + 1) * levels)
+            copies[member + 1].wait()
+            low_ref[part] = held_ref[member, :, :HALO, :]
+            high_ref[part] = held_ref[member, :, tile_rows - HALO:, :]
+        copies[0].wait()
+        low_ref[extra] = diff_ref[:HALO, :]
+        high_ref[extra] = diff_ref[tile_rows - HALO:, :]
+
+    @pl.when(odd)
+    def _():
+        give(second_ref, first_ref)
+
+    @pl.when(jnp.logical_not(odd))
+    def _():
+        give(first_ref, second_ref)
+
+
+def forecast(place_ref, x_hbm, diff_hbm, first_hbm, second_hbm, onehot_ref, pick_ref, prior_ref, out_hbm,
              wide_ref, own_ref, pair_ref, diff_ref, diff_sems, in_sems, out_sems):
     members, levels, tile_rows, width = x_hbm.shape
     heights = levels // V
@@ -133,7 +151,9 @@
     extra = members * levels
     top, own, bottom = pl.ds(0, HALO), pl.ds(HALO, tile_rows), pl.ds(HALO + tile_rows, HALO)
 
-    def arrivals(member):
+    odd = place_ref[2] == 1
+
+    def arrivals(member, low_hbm, high_hbm):
         part = pl.ds(member * levels, levels)
         return [
             pltpu.make_async_copy(x_hbm.at[member], wide_ref.at[member, :, own], in_sems.at[member, 0]),
@@ -144,18 +164,28 @@
     def departure(member):
         return pltpu.make_async_copy(own_ref.at[:, member], out_hbm.at[:, member], out_sems.at[member])
 
-    diffs = [
-        pltpu.make_async_copy(diff_hbm, diff_ref.at[own], diff_sems.at[0]),
-        pltpu.make_async_copy(low_hbm.at[extra], diff_ref.at[top], diff_sems.at[1]),
-        pltpu.make_async_copy(high_hbm.at[extra], diff_ref.at[bottom], diff_sems.at[2]),
-    ]
-    for copy in diffs:
-        copy.start()
-    for member in range(members):
-        for copy in arrivals(member):
+    def take(low_hbm, high_hbm):
+        diffs = [
+            pltpu.make_async_copy(diff_hbm, diff_ref.at[own], diff_sems.at[0]),
+            pltpu.make_async_copy(low_hbm.at[extra], diff_ref.at[top], diff_sems.at[1]),
+            pltpu.make_async_copy(high_hbm.at[extra], diff_ref.at[bottom], diff_sems.at[2]),
+        ]
+        for copy in diffs:
             copy.start()
-    for copy in diffs:
-        copy.wait()
+        for member in range(members):
+            for copy in arrivals(member, low_hbm, high_hbm):
+                copy.start()
+        for copy in diffs:
+            copy.wait()
+
+    @pl.when(odd)
+    def _():
+        take(second_hbm, first_hbm)
+
+    @pl.when(jnp.logical_not(odd))
+    def _():
+        take(first_hbm, second_hbm)
+
     diff = diff_ref[...]
     keep = 1.0 - 4.0 * diff
     upper = lax.broadcasted_iota(jnp.int32, (deep, width), 0) < tile_rows
@@ -173,7 +203,7 @@
 
     @pl.loop(0, members)
     def _(member):
-        for copy in arrivals(member):
+        for copy in arrivals(member, first_hbm, second_hbm):
             copy.wait()
         done = []
         for height in range(heights):
@@ -273,31 +303,33 @@
     tiles = lax.axis_size(space)
     planes = lax.axis_size("z")
     own_level = lax.axis_index(mem)
-    place = jnp.stack([lax.axis_index(space) * tile_rows, own_level]).astype(jnp.int32)
+    tile = lax.axis_index(space)
+    place = jnp.stack([tile * tile_rows, own_level, tile % 2]).astype(jnp.int32)
     cells = tile_rows * width
     shape = jax.ShapeDtypeStruct
     f32 = jnp.float32
 
     extra = members * levels
-    flat = ensemble.reshape(extra, tile_rows, width)
-    up, down = pl.pallas_call(
+    smem = [pl.BlockSpec(memory_space=pltpu.SMEM)]
+    first, second = pl.pallas_call(
         edges,
-        out_shape=[
-            shape((extra + 1, HALO, width), f32),
-            shape((extra + 1, HALO, width), f32),
-        ],
-        in_specs=hbm_specs(2),
+        out_shape=[pltpu.VMEM((extra + 1, HALO, width), f32)] * 2,
+        in_specs=smem + hbm_specs(2),
         out_specs=vmem_specs(2),
         scratch_shapes=[
-            pltpu.VMEM((extra, tile_rows, width), f32),
+            pltpu.VMEM(ensemble.shape, f32),
             pltpu.VMEM((tile_rows, width), f32),
-            pltpu.SemaphoreType.DMA((2,)),
+            pltpu.SemaphoreType.DMA((members + 1,)),
         ],
         compiler_params=params(8),
         name="edges",
-    )(*in_hbm(flat, diffusivity))
-    low = lax.ppermute(up, space, [(i, i + 1) for i in range(tiles - 1)])
-    high = lax.ppermute(down, space, [(i + 1, i) for i in range(tiles - 1)])
+    )(place, *in_hbm(ensemble, diffusivity))
+
+    def swap(message, start):
+        pairs = [(i, i + 1) for i in range(start, tiles - 1, 2)]
+        return lax.ppermute(message, space, pairs + [(j, i) for i, j in pairs])
+
+    first, second = swap(first, 1), swap(second, 0)
 
     line = lambda a: a.reshape(1, count)
     fields, weight, cross, onehot, pick = pl.pallas_call(
@@ -309,7 +341,7 @@
             shape((width, count), jnp.bfloat16),
             shape((V, 8, count), f32),
         ],
-        in_specs=[pl.BlockSpec(memory_space=pltpu.SMEM)] + hbm_specs(7),
+        in_specs=smem + hbm_specs(7),
         out_specs=vmem_specs(5),
         scratch_shapes=[
             pltpu.VMEM((4, 1, count), jnp.int32),
@@ -330,7 +362,7 @@
             shape((1, members * count), f32),
             pltpu.HBM((levels, members, tile_rows, width), f32),
         ],
-        in_specs=hbm_specs(4) + vmem_specs(2),
+        in_specs=smem + hbm_specs(4) + vmem_specs(2),
         out_specs=vmem_specs(1) + hbm_specs(1),
         scratch_shapes=[
             pltpu.VMEM((members, levels, deep, width), f32),
@@ -343,7 +375,7 @@
         ],
         compiler_params=params(16),
         name="forecast",
-    )(*in_hbm(ensemble, diffusivity), low, high, onehot, pick)
+    )(place, *in_hbm(ensemble, diffusivity), first, second, onehot, pick)
 
     reach = 2 * (LOC_RADIUS - 1)
     tiles_reached = -(-reach // tile_rows)

time: 70.9 us -> 68.6 us (0.968)
  blocking collectives: 21 us -> 16.9 us
  waiting for transfers between devices: 9.17 us -> 11.1 us
    all_to_all x1, blocking collectives: 21 us -> 16.9 us  [shards(): lax.all_to_all(jnp.broadcast_to(near[None], (size,) + near.shape), group,...]
    ppermute x2, waiting for transfers between devices: 5.49 us -> 7.44 us  [swap(): return lax.ppermute(message, space, pairs + [(j, i) for i, j in pairs])]
where the time goes in v3:
time: 68.6 us; the launch traced here: 68.2 us
  starting transfers between devices  26.3 us (38%)
  blocking collectives  16.9 us (25%)
  Pallas kernels  13.4 us (20%)
  waiting for transfers between devices  11.1 us (16%)
    all_to_all x1, blocking collectives, shards(): lax.all_to_all(jnp.broadcast_to(near[None], (size,) + near.shape), group,...  16.9 us
    ppermute x2, starting transfers between devices, swap(): return lax.ppermute(message, space, pairs + [(j, i) for i, j in pairs])  8.22 us
    ppermute x2, waiting for transfers between devices, swap(): return lax.ppermute(message, space, pairs + [(j, i) for i, j in pairs])  7.44 us
    ppermute x2, starting transfers between devices, shards(): lax.ppermute(prior, 'z', [(i + d, i) for i in range(planes - d)])  6.92 us
    all_to_all x1, starting transfers between devices, shards(): state = lax.all_to_all(state, mem, 0, 0, tiled=True)  6.17 us
    pallas_call x1, Pallas kernels, shards(): pl.pallas_call(forecast, out_shape=[shape((1, members * count), f32), plt...  6 us
    ppermute x2, starting transfers between devices, shards(): lax.ppermute(prior, 'z', [(i, i + d) for i in range(planes - d)])  5.02 us
    ppermute x2, waiting for transfers between devices, shards(): lax.ppermute(prior, 'z', [(i, i + d) for i in range(planes - d)])  3.67 us
  transfers between devices with their start and end apart: 7, of which 3 were waited for; matrix products, arithmetic and copies ran while one was open for 0% of the time, Pallas kernels for 4%

profile of v3, /device:TPU:385, one launch (start us, length us, event | category | flops | bytes accessed | tf_op | source)
XLA Modules:
  0.0 68.2 jit_solution(5599531123352118857)
XLA Ops:
  0.0 0.1 pad_add_fusion.place_ref.refs_0_
  0.1 1.9 %edges.1 = (f32[81,2,640]{2,1,0:T(2,128)S(1)}, f32[81,2,640]{2,1,0:T(2,128)S(1)}) custom-call(s32[3]{0:T(128)S(1)} %pad_add_fusion.place_ref.refs_0_, f32[10,8,4,640]{3,2,1,0:T(4,128)} %x_hbm.3, f32[4,640]{1,0:T(4,128)} %diff_hbm.3), custom_call_target="tpu_custom_call" | custom-call | tf_op jit(solution)/shard_map/edges/pallas_call | solution.py:314
  2.0 6.3 %collective-permute-start = (f32[81,2,640]{2,1,0:T(2,128)S(1)}, f32[81,2,640]{2,1,0:T(2,128)S(1)}, u32[]{:S(2)}, u32[]{:S(2)}) collective-permute-start(f32[81,2,640]{2,1,0:T(2,128)S(1)} %get-tuple-element.16), channel_id=1, source_target_pairs={{1,2},{3,4},{5,6},{7,8},{9,10},{11,12},{13,14},{15,16},{17,18},{19... | collective-permute-start | bytes 1244168 | tf_op jit(solution)/shard_map/ppermute | solution.py:330
  8.3 1.9 %collective-permute-start.1 = (f32[81,2,640]{2,1,0:T(2,128)S(1)}, f32[81,2,640]{2,1,0:T(2,128)S(1)}, u32[]{:S(2)}, u32[]{:S(2)}) collective-permute-start(f32[81,2,640]{2,1,0:T(2,128)S(1)} %get-tuple-element.17), channel_id=1, source_target_pairs={{0,1},{2,3},{4,5},{6,7},{8,9},{10,11},{12,13},{14,15},{16,17},{18,... | collective-permute-start | bytes 1244168 | tf_op jit(solution)/shard_map/ppermute | solution.py:330
  10.2 2.6 %prepare.1 = (f32[8,256]{1,0:T(8,128)S(1)}, f32[256,2560]{1,0:T(8,128)S(1)}, f32[128,128]{1,0:T(8,128)S(1)}, bf16[640,256]{1,0:T(8,128)(2,1)S(1)}, f32[4,8,256]{2,1,0:T(8,128)S(1)}) custom-call(s32[3]{0:T(128)S(1)} %pad_add_fusion.place_ref.refs_0_, s32[1,256]{1,0:T(1,128)} %bitcast.16, s32[1,256]{1,0:T(1,128)} %bitcast.17, s32[1,256]{1,0:T(1,128)} %bitcast.18, ...), custom_call_target="tpu_custom_call" | custom-call | flops 10000000 | bytes 4000000 | tf_op jit(solution)/shard_map/prepare/pallas_call | solution.py:335
  12.9 4.8 %collective-permute-done.first_hbm = f32[81,2,640]{2,1,0:T(2,128)S(1)} collective-permute-done((f32[81,2,640]{2,1,0:T(2,128)S(1)}, f32[81,2,640]{2,1,0:T(2,128)S(1)}, u32[]{:S(2)}, u32[]{:S(2)}) %collective-permute-start) | collective-permute-done | bytes 414752 | tf_op jit(solution)/shard_map/ppermute | solution.py:330
  17.6 2.7 %collective-permute-done.1.second_hbm = f32[81,2,640]{2,1,0:T(2,128)S(1)} collective-permute-done((f32[81,2,640]{2,1,0:T(2,128)S(1)}, f32[81,2,640]{2,1,0:T(2,128)S(1)}, u32[]{:S(2)}, u32[]{:S(2)}) %collective-permute-start.1) | collective-permute-done | bytes 414752 | tf_op jit(solution)/shard_map/ppermute | solution.py:330
  20.3 6.0 %forecast.1 = (f32[1,2560]{1,0:T(1,128)S(1)}, f32[8,10,4,640]{3,2,1,0:T(4,128)}) custom-call(s32[3]{0:T(128)S(1)} %pad_add_fusion.place_ref.refs_0_, f32[10,8,4,640]{3,2,1,0:T(4,128)} %x_hbm.3, f32[4,640]{1,0:T(4,128)} %diff_hbm.3, f32[81,2,640]{2,1,0:T(2,128)S(1)} %collective-permute-done.first_hbm, f32[81,2,640]{2,1,0:T(2,128)S(1)} %collective-permute-done.1.second_hbm, ...), custom_call_target="tpu_custom_call" | custom-call | tf_op jit(solution)/shard_map/forecast/pallas_call | solution.py:359
  26.3 6.2 %all-to-all-start = ((f32[8,10,4,640]{3,2,1,0:T(4,128)}), f32[8,10,4,640]{3,2,1,0:T(4,128)S(1)}, u32[]{:S(2)}, u32[]{:S(2)}) async-start(f32[8,10,4,640]{3,2,1,0:T(4,128)} %get-tuple-element.21), calls=%async_computation | async-start | bytes 1638400 | tf_op jit(solution)/shard_map/all_to_all | solution.py:388
  32.5 3.1 %collective-permute-start.5 = (f32[1,2560]{1,0:T(1,128)S(1)}, f32[1,2560]{1,0:T(1,128)S(1)}, u32[]{:S(2)}, u32[]{:S(2)}) collective-permute-start(f32[1,2560]{1,0:T(1,128)S(1)} %get-tuple-element.20), channel_id=1, source_target_pairs={{8,0},{12,4},{16,8},{20,12},{24,16},{28,20},{32,24},{36,28},{40,32... | collective-permute-start | bytes 30728 | tf_op jit(solution)/shard_map/ppermute | solution.py:387
  35.6 3.1 %collective-permute-start.4 = (f32[1,2560]{1,0:T(1,128)S(1)}, f32[1,2560]{1,0:T(1,128)S(1)}, u32[]{:S(2)}, u32[]{:S(2)}) collective-permute-start(f32[1,2560]{1,0:T(1,128)S(1)} %get-tuple-element.20), channel_id=1, source_target_pairs={{0,8},{4,12},{8,16},{12,20},{16,24},{20,28},{24,32},{28,36},{32,40... | collective-permute-start | bytes 30728 | tf_op jit(solution)/shard_map/ppermute | solution.py:386
  38.7 3.9 %collective-permute-start.3 = (f32[1,2560]{1,0:T(1,128)S(1)}, f32[1,2560]{1,0:T(1,128)S(1)}, u32[]{:S(2)}, u32[]{:S(2)}) collective-permute-start(f32[1,2560]{1,0:T(1,128)S(1)} %get-tuple-element.20), channel_id=1, source_target_pairs={{4,0},{8,4},{12,8},{16,12},{20,16},{24,20},{28,24},{32,28},{36,32}... | collective-permute-start | bytes 30728 | tf_op jit(solution)/shard_map/ppermute | solution.py:387
  42.5 1.9 %collective-permute-start.2 = (f32[1,2560]{1,0:T(1,128)S(1)}, f32[1,2560]{1,0:T(1,128)S(1)}, u32[]{:S(2)}, u32[]{:S(2)}) collective-permute-start(f32[1,2560]{1,0:T(1,128)S(1)} %get-tuple-element.20), channel_id=1, source_target_pairs={{0,4},{4,8},{8,12},{12,16},{16,20},{20,24},{24,28},{28,32},{32,36}... | collective-permute-start | bytes 30728 | tf_op jit(solution)/shard_map/ppermute | solution.py:386
  44.5 0.0 collective-permute-done.5
  44.5 0.0 collective-permute-done.4
  44.5 0.0 collective-permute-done.3
  44.5 3.7 %collective-permute-done.2 = f32[1,2560]{1,0:T(1,128)S(1)} collective-permute-done((f32[1,2560]{1,0:T(1,128)S(1)}, f32[1,2560]{1,0:T(1,128)S(1)}, u32[]{:S(2)}, u32[]{:S(2)}) %collective-permute-start.2) | collective-permute-done | bytes 10272 | tf_op jit(solution)/shard_map/ppermute | solution.py:386
  48.2 0.0 all-to-all-done
  48.2 0.2 broadcast_in_dim.12
  48.4 16.9 %all_to_all.10 = f32[32,1,2560]{2,1,0:T(1,128)S(1)} all-to-all(f32[32,1,2560]{2,1,0:T(1,128)S(1)} %broadcast_in_dim.12), channel_id=1, replica_groups=mesh['x'=4,'core'=2,'z'=16,'y'=4] {'x','core','y'}, dimensions={0} | all-to-all | bytes 655360 | tf_op jit(solution)/shard_map/all_to_all | solution.py:392
  65.3 2.8 %analyse.1 = f32[80,4,640]{2,1,0:T(4,128)} custom-call(f32[80,4,640]{2,1,0:T(4,128)S(1)} %bitcast.14, f32[8,4,1,2560]{3,2,1,0:T(1,128)S(1)} %bitcast.15, f32[8,256]{1,0:T(8,128)S(1)} %get-tuple-element.24.fields_ref, f32[256,2560]{1,0:T(8,128)S(1)} %get-tuple-element.25.weight_ref, f32[128,128]{1,0:T(8,128)S(1)} %get-tuple-element.26.cross_ref), custom_call_target="tpu_custom_call" | custom-call | tf_op jit(solution)/shard_map/analyse/pallas_call | solution.py:398
  (2 shorter events, 0.1 us)
Async XLA Ops:
  2.0 15.7 %collective-permute-start = (f32[81,2,640]{2,1,0:T(2,128)S(1)}, f32[81,2,640]{2,1,0:T(2,128)S(1)}, u32[]{:S(2)}, u32[]{:S(2)}) collective-permute-start(f32[81,2,640]{2,1,0:T(2,128)S(1)} %get-tuple-element.16), channel_id=1, source_target_pairs={{1,2},{3,4},{5,6},{7,8},{9,10},{11,12},{13,14},{15,16},{17,18},{19... | collective-permute-start | bytes 1244168 | tf_op jit(solution)/shard_map/ppermute | solution.py:330
  8.3 12.0 %collective-permute-start.1 = (f32[81,2,640]{2,1,0:T(2,128)S(1)}, f32[81,2,640]{2,1,0:T(2,128)S(1)}, u32[]{:S(2)}, u32[]{:S(2)}) collective-permute-start(f32[81,2,640]{2,1,0:T(2,128)S(1)} %get-tuple-element.17), channel_id=1, source_target_pairs={{0,1},{2,3},{4,5},{6,7},{8,9},{10,11},{12,13},{14,15},{16,17},{18,... | collective-permute-start | bytes 1244168 | tf_op jit(solution)/shard_map/ppermute | solution.py:330
  26.3 21.9 %all-to-all-start = ((f32[8,10,4,640]{3,2,1,0:T(4,128)}), f32[8,10,4,640]{3,2,1,0:T(4,128)S(1)}, u32[]{:S(2)}, u32[]{:S(2)}) async-start(f32[8,10,4,640]{3,2,1,0:T(4,128)} %get-tuple-element.21), calls=%async_computation | async-start | bytes 1638400 | tf_op jit(solution)/shard_map/all_to_all | solution.py:388
  32.5 12.0 %collective-permute-start.5 = (f32[1,2560]{1,0:T(1,128)S(1)}, f32[1,2560]{1,0:T(1,128)S(1)}, u32[]{:S(2)}, u32[]{:S(2)}) collective-permute-start(f32[1,2560]{1,0:T(1,128)S(1)} %get-tuple-element.20), channel_id=1, source_target_pairs={{8,0},{12,4},{16,8},{20,12},{24,16},{28,20},{32,24},{36,28},{40,32... | collective-permute-start | bytes 30728 | tf_op jit(solution)/shard_map/ppermute | solution.py:387
  35.6 8.9 %collective-permute-start.4 = (f32[1,2560]{1,0:T(1,128)S(1)}, f32[1,2560]{1,0:T(1,128)S(1)}, u32[]{:S(2)}, u32[]{:S(2)}) collective-permute-start(f32[1,2560]{1,0:T(1,128)S(1)} %get-tuple-element.20), channel_id=1, source_target_pairs={{0,8},{4,12},{8,16},{12,20},{16,24},{20,28},{24,32},{28,36},{32,40... | collective-permute-start | bytes 30728 | tf_op jit(solution)/shard_map/ppermute | solution.py:386
  38.7 5.8 %collective-permute-start.3 = (f32[1,2560]{1,0:T(1,128)S(1)}, f32[1,2560]{1,0:T(1,128)S(1)}, u32[]{:S(2)}, u32[]{:S(2)}) collective-permute-start(f32[1,2560]{1,0:T(1,128)S(1)} %get-tuple-element.20), channel_id=1, source_target_pairs={{4,0},{8,4},{12,8},{16,12},{20,16},{24,20},{28,24},{32,28},{36,32}... | collective-permute-start | bytes 30728 | tf_op jit(solution)/shard_map/ppermute | solution.py:387
  42.5 5.6 %collective-permute-start.2 = (f32[1,2560]{1,0:T(1,128)S(1)}, f32[1,2560]{1,0:T(1,128)S(1)}, u32[]{:S(2)}, u32[]{:S(2)}) collective-permute-start(f32[1,2560]{1,0:T(1,128)S(1)} %get-tuple-element.20), channel_id=1, source_target_pairs={{0,4},{4,8},{8,12},{12,16},{16,20},{20,24},{24,28},{28,32},{32,36}... | collective-permute-start | bytes 30728 | tf_op jit(solution)/shard_map/ppermute | solution.py:386

commit v4 on v3

--- a/solution.py
+++ b/solution.py
@@ -108,11 +108,12 @@
     onehot_ref[...] = (lon_id == lons).astype(jnp.bfloat16)
     heights = levels // V
     slot = lax.broadcasted_iota(jnp.int32, (8, count), 0)
-    height = slot // tile_rows
-    inside = rows - tile_start.astype(jnp.float32) == (slot - height * tile_rows).astype(jnp.float32)
-    for v in range(V):
-        there = levs == (v * heights + height).astype(jnp.float32)
-        pick_ref[v] = jnp.where(inside & there, 1.0, 0.0)
+    half = slot // tile_rows
+    inside = rows - tile_start.astype(jnp.float32) == (slot - half * tile_rows).astype(jnp.float32)
+    for height in range(heights):
+        for p in range(V // 2):
+            there = levs == ((2 * p + half) * heights + height).astype(jnp.float32)
+            pick_ref[height * (V // 2) + p] = jnp.where(inside & there, 1.0, 0.0)
 
 
 def edges(place_ref, x_hbm, diff_hbm, first_ref, second_ref, held_ref, diff_ref, sems):
@@ -190,32 +191,43 @@
     keep = 1.0 - 4.0 * diff
     upper = lax.broadcasted_iota(jnp.int32, (deep, width), 0) < tile_rows
 
-    def sub_step(fields):
-        push_u, push_w = ADVECT * fields[0], ADVECT * fields[1]
-        from_east, from_west = diff - push_u, diff + push_u
-        from_north, from_south = diff - push_w, diff + push_w
-        return [
+    def spread(diff, wind_u, wind_w):
+        push_u, push_w = ADVECT * wind_u, ADVECT * wind_w
+        return diff - push_u, diff + push_u, diff - push_w, diff + push_w
+
+    def moved(keep, ways, q, north, south):
+        from_east, from_west, from_north, from_south = ways
+        return (
             keep * q
             + (from_east * pltpu.roll(q, width - 1, 1) + from_west * pltpu.roll(q, 1, 1))
-            + (from_north * pltpu.roll(q, deep - 1, 0) + from_south * pltpu.roll(q, 1, 0))
-            for q in fields
-        ]
+            + (from_north * north + from_south * south)
+        )
+
+    def paired(a, b, shift):
+        return jnp.where(
+            upper,
+            pltpu.roll(a, deep - HALO - shift, 0),
+            pltpu.roll(b, tile_rows - HALO - shift, 0),
+        )
+
+    two_diff, two_keep = paired(diff, diff, 0), paired(keep, keep, 0)
 
     @pl.loop(0, members)
     def _(member):
         for copy in arrivals(member, first_hbm, second_hbm):
             copy.wait()
-        done = []
         for height in range(heights):
-            fields = sub_step(sub_step([wide_ref[member, v * heights + height] for v in range(V)]))
-            for v in range(V):
-                own_ref[v * heights + height, member] = fields[v][HALO:HALO + tile_rows]
-            done.append(fields)
+            q = [wide_ref[member, v * heights + height] for v in range(V)]
+            ways = spread(diff, q[0], q[1])
+            q = [moved(keep, ways, a, pltpu.roll(a, deep - 1, 0), pltpu.roll(a, 1, 0)) for a in q]
+            ways = spread(two_diff, paired(q[0], q[0], 0), paired(q[1], q[1], 0))
+            for p in range(V // 2):
+                a, b = q[2 * p], q[2 * p + 1]
+                pair = moved(two_keep, ways, paired(a, b, 0), paired(a, b, 1), paired(a, b, -1))
+                pair_ref[height * (V // 2) + p, member] = pair
+                own_ref[2 * p * heights + height, member] = pair[:tile_rows]
+                own_ref[(2 * p + 1) * heights + height, member] = pair[tile_rows:]
         departure(member).start()
-        for v in range(V):
-            pair_ref[v, member] = jnp.where(
-                upper, pltpu.roll(done[0][v], deep - HALO, 0), pltpu.roll(done[1][v], HALO, 0)
-            )
 
     count = onehot_ref.shape[1]
     total = jnp.zeros((members, deep, count), jnp.float32)
@@ -267,15 +279,17 @@
 
 def analyse(x_ref, prior_ref, fields_ref, weight_ref, cross_ref, out_ref, scratch):
     members, tile_rows, width = x_ref.shape
-    planes, tiles, _, _ = prior_ref.shape
+    cores, tiles, chips, _, _ = prior_ref.shape
+    planes = cores * chips
     count = fields_ref.shape[1]
     share = members // planes
     for i in range(planes):
+        core, chip = i % cores, i // cores
         for m in range(share):
             at = slice(m * count, (m + 1) * count)
-            line = prior_ref[i, 0, :, at]
+            line = prior_ref[core, 0, chip, :, at]
             for t in range(1, tiles):
-                line = line + prior_ref[i, t, :, at]
+                line = line + prior_ref[core, t, chip, :, at]
             scratch[i * share + m:i * share + m + 1, :] = line
     prior = scratch[...]
     values = fields_ref[3:4]
@@ -387,12 +401,12 @@
         near = near + lax.ppermute(prior, "z", [(i + d, i) for i in range(planes - d)])
     state = lax.all_to_all(state, mem, 0, 0, tiled=True)
     near, state = lax.optimization_barrier((near, state))
-    group = mem + ("y",)
+    group = ("core", "y", "x")
     size = lax.axis_size(group)
     spread = lax.all_to_all(
         jnp.broadcast_to(near[None], (size,) + near.shape), group, 0, 0, tiled=True
     )
-    spread = spread.reshape((size // rows_of_tiles, rows_of_tiles) + near.shape)
+    spread = spread.reshape(tuple(lax.axis_size(a) for a in group) + near.shape)
     state = state.reshape(-1, tile_rows, width)
 
     out = pl.pallas_call(

time: 68.6 us -> 68 us (level)
  no operation moved by 1% of the time
where the time goes in v4:
time: 68 us; the launch traced here: 67 us
  starting transfers between devices  26.3 us (39%)
  blocking collectives  16.3 us (24%)
  Pallas kernels  12.9 us (19%)
  waiting for transfers between devices  11.1 us (16%)
    all_to_all x1, blocking collectives, shards(): lax.all_to_all(jnp.broadcast_to(near[None], (size,) + near.shape), group,...  16.3 us
    ppermute x2, starting transfers between devices, swap(): return lax.ppermute(message, space, pairs + [(j, i) for i, j in pairs])  8.22 us
    ppermute x2, waiting for transfers between devices, swap(): return lax.ppermute(message, space, pairs + [(j, i) for i, j in pairs])  7.44 us
    ppermute x2, starting transfers between devices, shards(): lax.ppermute(prior, 'z', [(i + d, i) for i in range(planes - d)])  6.92 us
    all_to_all x1, starting transfers between devices, shards(): state = lax.all_to_all(state, mem, 0, 0, tiled=True)  6.17 us
    pallas_call x1, Pallas kernels, shards(): pl.pallas_call(forecast, out_shape=[shape((1, members * count), f32), plt...  5.47 us
    ppermute x2, starting transfers between devices, shards(): lax.ppermute(prior, 'z', [(i, i + d) for i in range(planes - d)])  5.02 us
    ppermute x2, waiting for transfers between devices, shards(): lax.ppermute(prior, 'z', [(i, i + d) for i in range(planes - d)])  3.67 us
  transfers between devices with their start and end apart: 7, of which 3 were waited for; matrix products, arithmetic and copies ran while one was open for 0% of the time, Pallas kernels for 4%

profile of v4, /device:TPU:385, one launch (start us, length us, event | category | flops | bytes accessed | tf_op | source)
XLA Modules:
  0.0 67.0 jit_solution(14619798467471764250)
XLA Ops:
  0.0 0.1 pad_add_fusion.place_ref.refs_0_
  0.1 1.9 %edges.1 = (f32[81,2,640]{2,1,0:T(2,128)S(1)}, f32[81,2,640]{2,1,0:T(2,128)S(1)}) custom-call(s32[3]{0:T(128)S(1)} %pad_add_fusion.place_ref.refs_0_, f32[10,8,4,640]{3,2,1,0:T(4,128)} %x_hbm.3, f32[4,640]{1,0:T(4,128)} %diff_hbm.3), custom_call_target="tpu_custom_call" | custom-call | tf_op jit(solution)/shard_map/edges/pallas_call | solution.py:328
  2.0 6.3 %collective-permute-start = (f32[81,2,640]{2,1,0:T(2,128)S(1)}, f32[81,2,640]{2,1,0:T(2,128)S(1)}, u32[]{:S(2)}, u32[]{:S(2)}) collective-permute-start(f32[81,2,640]{2,1,0:T(2,128)S(1)} %get-tuple-element.16), channel_id=1, source_target_pairs={{1,2},{3,4},{5,6},{7,8},{9,10},{11,12},{13,14},{15,16},{17,18},{19... | collective-permute-start | bytes 1244168 | tf_op jit(solution)/shard_map/ppermute | solution.py:344
  8.3 1.9 %collective-permute-start.1 = (f32[81,2,640]{2,1,0:T(2,128)S(1)}, f32[81,2,640]{2,1,0:T(2,128)S(1)}, u32[]{:S(2)}, u32[]{:S(2)}) collective-permute-start(f32[81,2,640]{2,1,0:T(2,128)S(1)} %get-tuple-element.17), channel_id=1, source_target_pairs={{0,1},{2,3},{4,5},{6,7},{8,9},{10,11},{12,13},{14,15},{16,17},{18,... | collective-permute-start | bytes 1244168 | tf_op jit(solution)/shard_map/ppermute | solution.py:344
  10.2 2.6 %prepare.1 = (f32[8,256]{1,0:T(8,128)S(1)}, f32[256,2560]{1,0:T(8,128)S(1)}, f32[128,128]{1,0:T(8,128)S(1)}, bf16[640,256]{1,0:T(8,128)(2,1)S(1)}, f32[4,8,256]{2,1,0:T(8,128)S(1)}) custom-call(s32[3]{0:T(128)S(1)} %pad_add_fusion.place_ref.refs_0_, s32[1,256]{1,0:T(1,128)} %bitcast.16, s32[1,256]{1,0:T(1,128)} %bitcast.17, s32[1,256]{1,0:T(1,128)} %bitcast.18, ...), custom_call_target="tpu_custom_call" | custom-call | flops 10000000 | bytes 4000000 | tf_op jit(solution)/shard_map/prepare/pallas_call | solution.py:349
  12.9 4.8 %collective-permute-done.first_hbm = f32[81,2,640]{2,1,0:T(2,128)S(1)} collective-permute-done((f32[81,2,640]{2,1,0:T(2,128)S(1)}, f32[81,2,640]{2,1,0:T(2,128)S(1)}, u32[]{:S(2)}, u32[]{:S(2)}) %collective-permute-start) | collective-permute-done | bytes 414752 | tf_op jit(solution)/shard_map/ppermute | solution.py:344
  17.6 2.7 %collective-permute-done.1.second_hbm = f32[81,2,640]{2,1,0:T(2,128)S(1)} collective-permute-done((f32[81,2,640]{2,1,0:T(2,128)S(1)}, f32[81,2,640]{2,1,0:T(2,128)S(1)}, u32[]{:S(2)}, u32[]{:S(2)}) %collective-permute-start.1) | collective-permute-done | bytes 414752 | tf_op jit(solution)/shard_map/ppermute | solution.py:344
  20.3 5.5 %forecast.1 = (f32[1,2560]{1,0:T(1,128)S(1)}, f32[8,10,4,640]{3,2,1,0:T(4,128)}) custom-call(s32[3]{0:T(128)S(1)} %pad_add_fusion.place_ref.refs_0_, f32[10,8,4,640]{3,2,1,0:T(4,128)} %x_hbm.3, f32[4,640]{1,0:T(4,128)} %diff_hbm.3, f32[81,2,640]{2,1,0:T(2,128)S(1)} %collective-permute-done.first_hbm, f32[81,2,640]{2,1,0:T(2,128)S(1)} %collective-permute-done.1.second_hbm, ...), custom_call_target="tpu_custom_call" | custom-call | tf_op jit(solution)/shard_map/forecast/pallas_call | solution.py:373
  25.8 6.2 %all-to-all-start = ((f32[8,10,4,640]{3,2,1,0:T(4,128)}), f32[8,10,4,640]{3,2,1,0:T(4,128)S(1)}, u32[]{:S(2)}, u32[]{:S(2)}) async-start(f32[8,10,4,640]{3,2,1,0:T(4,128)} %get-tuple-element.21), calls=%async_computation | async-start | bytes 1638400 | tf_op jit(solution)/shard_map/all_to_all | solution.py:402
  32.0 3.1 %collective-permute-start.5 = (f32[1,2560]{1,0:T(1,128)S(1)}, f32[1,2560]{1,0:T(1,128)S(1)}, u32[]{:S(2)}, u32[]{:S(2)}) collective-permute-start(f32[1,2560]{1,0:T(1,128)S(1)} %get-tuple-element.20), channel_id=1, source_target_pairs={{8,0},{12,4},{16,8},{20,12},{24,16},{28,20},{32,24},{36,28},{40,32... | collective-permute-start | bytes 30728 | tf_op jit(solution)/shard_map/ppermute | solution.py:401
  35.0 3.1 %collective-permute-start.4 = (f32[1,2560]{1,0:T(1,128)S(1)}, f32[1,2560]{1,0:T(1,128)S(1)}, u32[]{:S(2)}, u32[]{:S(2)}) collective-permute-start(f32[1,2560]{1,0:T(1,128)S(1)} %get-tuple-element.20), channel_id=1, source_target_pairs={{0,8},{4,12},{8,16},{12,20},{16,24},{20,28},{24,32},{28,36},{32,40... | collective-permute-start | bytes 30728 | tf_op jit(solution)/shard_map/ppermute | solution.py:400
  38.1 3.8 %collective-permute-start.3 = (f32[1,2560]{1,0:T(1,128)S(1)}, f32[1,2560]{1,0:T(1,128)S(1)}, u32[]{:S(2)}, u32[]{:S(2)}) collective-permute-start(f32[1,2560]{1,0:T(1,128)S(1)} %get-tuple-element.20), channel_id=1, source_target_pairs={{4,0},{8,4},{12,8},{16,12},{20,16},{24,20},{28,24},{32,28},{36,32}... | collective-permute-start | bytes 30728 | tf_op jit(solution)/shard_map/ppermute | solution.py:401
  42.0 1.9 %collective-permute-start.2 = (f32[1,2560]{1,0:T(1,128)S(1)}, f32[1,2560]{1,0:T(1,128)S(1)}, u32[]{:S(2)}, u32[]{:S(2)}) collective-permute-start(f32[1,2560]{1,0:T(1,128)S(1)} %get-tuple-element.20), channel_id=1, source_target_pairs={{0,4},{4,8},{8,12},{12,16},{16,20},{20,24},{24,28},{28,32},{32,36}... | collective-permute-start | bytes 30728 | tf_op jit(solution)/shard_map/ppermute | solution.py:400
  43.9 0.0 collective-permute-done.5
  43.9 0.0 collective-permute-done.4
  44.0 0.0 collective-permute-done.3
  44.0 3.7 %collective-permute-done.2 = f32[1,2560]{1,0:T(1,128)S(1)} collective-permute-done((f32[1,2560]{1,0:T(1,128)S(1)}, f32[1,2560]{1,0:T(1,128)S(1)}, u32[]{:S(2)}, u32[]{:S(2)}) %collective-permute-start.2) | collective-permute-done | bytes 10272 | tf_op jit(solution)/shard_map/ppermute | solution.py:400
  47.7 0.0 all-to-all-done
  47.7 0.2 broadcast_in_dim.12
  47.9 16.3 %all_to_all.10 = f32[32,1,2560]{2,1,0:T(1,128)S(1)} all-to-all(f32[32,1,2560]{2,1,0:T(1,128)S(1)} %broadcast_in_dim.12), channel_id=1, replica_groups=mesh['x'=4,'core'=2,'z'=16,'y'=4] {'core','y','x'}, dimensions={0} | all-to-all | bytes 655360 | tf_op jit(solution)/shard_map/all_to_all | solution.py:406
  64.2 2.8 %analyse.1 = f32[80,4,640]{2,1,0:T(4,128)} custom-call(f32[80,4,640]{2,1,0:T(4,128)S(1)} %bitcast.14, f32[2,4,4,1,2560]{4,3,2,1,0:T(1,128)S(1)} %bitcast.15, f32[8,256]{1,0:T(8,128)S(1)} %get-tuple-element.24.fields_ref, f32[256,2560]{1,0:T(8,128)S(1)} %get-tuple-element.25.weight_ref, f32[128,128]{1,0:T(8,128)S(1)} %get-tuple-element.26.cross_ref), custom_call_target="tpu_custom_call" | custom-call | tf_op jit(solution)/shard_map/analyse/pallas_call | solution.py:412
  (2 shorter events, 0.1 us)
Async XLA Ops:
  2.0 15.7 %collective-permute-start = (f32[81,2,640]{2,1,0:T(2,128)S(1)}, f32[81,2,640]{2,1,0:T(2,128)S(1)}, u32[]{:S(2)}, u32[]{:S(2)}) collective-permute-start(f32[81,2,640]{2,1,0:T(2,128)S(1)} %get-tuple-element.16), channel_id=1, source_target_pairs={{1,2},{3,4},{5,6},{7,8},{9,10},{11,12},{13,14},{15,16},{17,18},{19... | collective-permute-start | bytes 1244168 | tf_op jit(solution)/shard_map/ppermute | solution.py:344
  8.3 12.0 %collective-permute-start.1 = (f32[81,2,640]{2,1,0:T(2,128)S(1)}, f32[81,2,640]{2,1,0:T(2,128)S(1)}, u32[]{:S(2)}, u32[]{:S(2)}) collective-permute-start(f32[81,2,640]{2,1,0:T(2,128)S(1)} %get-tuple-element.17), channel_id=1, source_target_pairs={{0,1},{2,3},{4,5},{6,7},{8,9},{10,11},{12,13},{14,15},{16,17},{18,... | collective-permute-start | bytes 1244168 | tf_op jit(solution)/shard_map/ppermute | solution.py:344
  25.8 21.9 %all-to-all-start = ((f32[8,10,4,640]{3,2,1,0:T(4,128)}), f32[8,10,4,640]{3,2,1,0:T(4,128)S(1)}, u32[]{:S(2)}, u32[]{:S(2)}) async-start(f32[8,10,4,640]{3,2,1,0:T(4,128)} %get-tuple-element.21), calls=%async_computation | async-start | bytes 1638400 | tf_op jit(solution)/shard_map/all_to_all | solution.py:402
  32.0 12.0 %collective-permute-start.5 = (f32[1,2560]{1,0:T(1,128)S(1)}, f32[1,2560]{1,0:T(1,128)S(1)}, u32[]{:S(2)}, u32[]{:S(2)}) collective-permute-start(f32[1,2560]{1,0:T(1,128)S(1)} %get-tuple-element.20), channel_id=1, source_target_pairs={{8,0},{12,4},{16,8},{20,12},{24,16},{28,20},{32,24},{36,28},{40,32... | collective-permute-start | bytes 30728 | tf_op jit(solution)/shard_map/ppermute | solution.py:401
  35.0 8.9 %collective-permute-start.4 = (f32[1,2560]{1,0:T(1,128)S(1)}, f32[1,2560]{1,0:T(1,128)S(1)}, u32[]{:S(2)}, u32[]{:S(2)}) collective-permute-start(f32[1,2560]{1,0:T(1,128)S(1)} %get-tuple-element.20), channel_id=1, source_target_pairs={{0,8},{4,12},{8,16},{12,20},{16,24},{20,28},{24,32},{28,36},{32,40... | collective-permute-start | bytes 30728 | tf_op jit(solution)/shard_map/ppermute | solution.py:400
  38.1 5.8 %collective-permute-start.3 = (f32[1,2560]{1,0:T(1,128)S(1)}, f32[1,2560]{1,0:T(1,128)S(1)}, u32[]{:S(2)}, u32[]{:S(2)}) collective-permute-start(f32[1,2560]{1,0:T(1,128)S(1)} %get-tuple-element.20), channel_id=1, source_target_pairs={{4,0},{8,4},{12,8},{16,12},{20,16},{24,20},{28,24},{32,28},{36,32}... | collective-permute-start | bytes 30728 | tf_op jit(solution)/shard_map/ppermute | solution.py:401
  42.0 5.6 %collective-permute-start.2 = (f32[1,2560]{1,0:T(1,128)S(1)}, f32[1,2560]{1,0:T(1,128)S(1)}, u32[]{:S(2)}, u32[]{:S(2)}) collective-permute-start(f32[1,2560]{1,0:T(1,128)S(1)} %get-tuple-element.20), channel_id=1, source_target_pairs={{0,4},{4,8},{8,12},{12,16},{16,20},{20,24},{24,28},{28,32},{32,36}... | collective-permute-start | bytes 30728 | tf_op jit(solution)/shard_map/ppermute | solution.py:400

commit v5 on v4

--- a/solution.py
+++ b/solution.py
@@ -144,8 +144,8 @@
         give(first_ref, second_ref)
 
 
-def forecast(place_ref, x_hbm, diff_hbm, first_hbm, second_hbm, onehot_ref, pick_ref, prior_ref, out_hbm,
-             wide_ref, own_ref, pair_ref, diff_ref, diff_sems, in_sems, out_sems):
+def forecast(place_ref, x_hbm, diff_hbm, first_hbm, second_hbm, pair_ref, out_hbm,
+             wide_ref, own_ref, diff_ref, diff_sems, in_sems, out_sems):
     members, levels, tile_rows, width = x_hbm.shape
     heights = levels // V
     deep = tile_rows + 2 * HALO
@@ -229,6 +229,12 @@
                 own_ref[(2 * p + 1) * heights + height, member] = pair[tile_rows:]
         departure(member).start()
 
+    for member in range(members):
+        departure(member).wait()
+
+
+def gather(pair_ref, onehot_ref, pick_ref, prior_ref):
+    _, members, deep, width = pair_ref.shape
     count = onehot_ref.shape[1]
     total = jnp.zeros((members, deep, count), jnp.float32)
     for v in range(V):
@@ -242,8 +248,6 @@
     prior = jnp.sum(total, axis=1)
     for m in range(members):
         prior_ref[:, m * count:(m + 1) * count] = prior[m:m + 1]
-    for member in range(members):
-        departure(member).wait()
 
 
 def split(a):
@@ -370,18 +374,17 @@
                      line(obs_error), coupling))
 
     deep = tile_rows + 2 * HALO
-    prior, state = pl.pallas_call(
+    pairs, state = pl.pallas_call(
         forecast,
         out_shape=[
-            shape((1, members * count), f32),
+            pltpu.VMEM((V, members, deep, width), f32),
             pltpu.HBM((levels, members, tile_rows, width), f32),
         ],
-        in_specs=smem + hbm_specs(4) + vmem_specs(2),
+        in_specs=smem + hbm_specs(4),
         out_specs=vmem_specs(1) + hbm_specs(1),
         scratch_shapes=[
             pltpu.VMEM((members, levels, deep, width), f32),
             pltpu.VMEM((levels, members, tile_rows, width), f32),
-            pltpu.VMEM((V, members, deep, width), f32),
             pltpu.VMEM((deep, width), f32),
             pltpu.SemaphoreType.DMA((3,)),
             pltpu.SemaphoreType.DMA((members, 3)),
@@ -389,18 +392,33 @@
         ],
         compiler_params=params(16),
         name="forecast",
-    )(place, *in_hbm(ensemble, diffusivity), first, second, onehot, pick)
+    )(place, *in_hbm(ensemble, diffusivity), first, second)
+    prior = pl.pallas_call(
+        gather,
+        out_shape=shape((1, members * count), f32),
+        in_specs=vmem_specs(3),
+        out_specs=pl.BlockSpec(memory_space=pltpu.VMEM),
+        compiler_params=params(8),
+        cost_estimate=pl.CostEstimate(flops=20_000_000_000, bytes_accessed=60_000_000, transcendentals=0),
+        name="gather",
+    )(pairs, onehot, pick)
 
     reach = 2 * (LOC_RADIUS - 1)
     tiles_reached = -(-reach // tile_rows)
     rows_of_tiles = tiles // planes
     planes_reached = min(-(-tiles_reached // rows_of_tiles), planes - 1)
-    near = prior
+    core = lax.axis_index("core")
+    both = lax.all_gather(prior, "core", axis=0, tiled=True).reshape(1, -1)
+    near = jnp.where(core == 0, both, 0.0)
     for d in range(1, planes_reached + 1):
-        near = near + lax.ppermute(prior, "z", [(i, i + d) for i in range(planes - d)])
-        near = near + lax.ppermute(prior, "z", [(i + d, i) for i in range(planes - d)])
+        ways = [(i, i + d) for i in range(planes - d)]
+        ways += [(planes + i + d, planes + i) for i in range(planes - d)]
+        near = near + lax.ppermute(both, ("core", "z"), ways)
     state = lax.all_to_all(state, mem, 0, 0, tiled=True)
     near, state = lax.optimization_barrier((near, state))
+    near = lax.all_gather(near, "core", axis=0, tiled=True)
+    near = (near[0:1] + near[1:2]).reshape(2, -1)
+    near = jnp.where(core == 0, near[0:1], near[1:2])
     group = ("core", "y", "x")
     size = lax.axis_size(group)
     spread = lax.all_to_all(

time: 68 us -> 75.5 us (1.11)
  the two profiles are of different devices: /device:TPU:385 before, /device:TPU:1 now
where the time goes in v5:
time: 75.5 us; the launch traced here: 75.1 us
  starting transfers between devices  22.6 us (30%)
  blocking collectives  21.7 us (29%)
  waiting for transfers between devices  15.5 us (21%)
  Pallas kernels  13.5 us (18%)
  other arithmetic  0.91 us (1%)
  local copies, waits for them, and re-layouts  0.77 us (1%)
    all_to_all x1, blocking collectives, shards(): lax.all_to_all(jnp.broadcast_to(near[None], (size,) + near.shape), group,...  14.3 us
    all_to_all x1, starting transfers between devices, shards(): state = lax.all_to_all(state, mem, 0, 0, tiled=True)  12.8 us
    all_to_all x1, waiting for transfers between devices, shards(): state = lax.all_to_all(state, mem, 0, 0, tiled=True)  11.2 us
    ppermute x2, starting transfers between devices, swap(): return lax.ppermute(message, space, pairs + [(j, i) for i, j in pairs])  7.24 us
    pallas_call x1, Pallas kernels, shards(): pl.pallas_call(forecast, out_shape=[pltpu.VMEM((V, members, deep, width),...  5.23 us
    all_gather x1, blocking collectives, shards(): both = lax.all_gather(prior, 'core', axis=0, tiled=True).reshape(1, -1)  5.13 us
    ppermute x2, waiting for transfers between devices, swap(): return lax.ppermute(message, space, pairs + [(j, i) for i, j in pairs])  4.22 us
    pallas_call x1, Pallas kernels, shards(): pl.pallas_call(analyse, out_shape=shape(state.shape, f32), in_specs=vmem_...  2.84 us
  transfers between devices with their start and end apart: 5, of which 2 were waited for; matrix products, arithmetic and copies ran while one was open for 1% of the time, Pallas kernels for 4%

profile of v5, /device:TPU:1, one launch (start us, length us, event | category | flops | bytes accessed | tf_op | source)
XLA Modules:
  0.0 75.1 jit_solution(12445323837822817882)
XLA Ops:
  0.0 0.1 pad_add_fusion.place_ref.refs_0_
  0.1 1.9 %edges.1 = (f32[81,2,640]{2,1,0:T(2,128)S(1)}, f32[81,2,640]{2,1,0:T(2,128)S(1)}) custom-call(s32[3]{0:T(128)S(1)} %pad_add_fusion.place_ref.refs_0_, f32[10,8,4,640]{3,2,1,0:T(4,128)} %x_hbm.3, f32[4,640]{1,0:T(4,128)} %diff_hbm.3), custom_call_target="tpu_custom_call" | custom-call | tf_op jit(solution)/shard_map/edges/pallas_call | solution.py:332
  2.0 0.7 collective-permute-start
  2.7 6.6 %collective-permute-start.1 = (f32[81,2,640]{2,1,0:T(2,128)S(1)}, f32[81,2,640]{2,1,0:T(2,128)S(1)}, u32[]{:S(2)}, u32[]{:S(2)}) collective-permute-start(f32[81,2,640]{2,1,0:T(2,128)S(1)} %get-tuple-element.17), channel_id=1, source_target_pairs={{0,1},{2,3},{4,5},{6,7},{8,9},{10,11},{12,13},{14,15},{16,17},{18,... | collective-permute-start | bytes 1244168 | tf_op jit(solution)/shard_map/ppermute | solution.py:348
  9.2 2.6 %prepare.1 = (f32[8,256]{1,0:T(8,128)S(1)}, f32[256,2560]{1,0:T(8,128)S(1)}, f32[128,128]{1,0:T(8,128)S(1)}, bf16[640,256]{1,0:T(8,128)(2,1)S(1)}, f32[4,8,256]{2,1,0:T(8,128)S(1)}) custom-call(s32[3]{0:T(128)S(1)} %pad_add_fusion.place_ref.refs_0_, s32[1,256]{1,0:T(1,128)} %bitcast.26, s32[1,256]{1,0:T(1,128)} %bitcast.27, s32[1,256]{1,0:T(1,128)} %bitcast.28, ...), custom_call_target="tpu_custom_call" | custom-call | flops 10000000 | bytes 4000000 | tf_op jit(solution)/shard_map/prepare/pallas_call | solution.py:353
  11.9 0.0 collective-permute-done.first_hbm
  11.9 4.2 %collective-permute-done.1.second_hbm = f32[81,2,640]{2,1,0:T(2,128)S(1)} collective-permute-done((f32[81,2,640]{2,1,0:T(2,128)S(1)}, f32[81,2,640]{2,1,0:T(2,128)S(1)}, u32[]{:S(2)}, u32[]{:S(2)}) %collective-permute-start.1) | collective-permute-done | bytes 414752 | tf_op jit(solution)/shard_map/ppermute | solution.py:348
  16.1 5.2 %forecast.1 = (f32[4,10,8,640]{3,2,1,0:T(8,128)S(1)}, f32[8,10,4,640]{3,2,1,0:T(4,128)}) custom-call(s32[3]{0:T(128)S(1)} %pad_add_fusion.place_ref.refs_0_, f32[10,8,4,640]{3,2,1,0:T(4,128)} %x_hbm.3, f32[4,640]{1,0:T(4,128)} %diff_hbm.3, f32[81,2,640]{2,1,0:T(2,128)S(1)} %collective-permute-done.first_hbm, f32[81,2,640]{2,1,0:T(2,128)S(1)} %collective-permute-done.1.second_hbm), custom_call_target="tpu_custom_call" | custom-call | tf_op jit(solution)/shard_map/forecast/pallas_call | solution.py:377
  21.4 0.9 %gather.1 = f32[1,2560]{1,0:T(1,128)S(1)} custom-call(f32[4,10,8,640]{3,2,1,0:T(8,128)S(1)} %get-tuple-element.18.pair_ref, bf16[640,256]{1,0:T(8,128)(2,1)S(1)} %get-tuple-element.19.onehot_ref, f32[4,8,256]{2,1,0:T(8,128)S(1)} %get-tuple-element.20.pick_ref), custom_call_target="tpu_custom_call" | custom-call | flops 20000000000 | bytes 60000000 | tf_op jit(solution)/shard_map/gather/pallas_call | solution.py:396
  22.2 5.1 %all-gather = f32[2,1,2560]{2,1,0:T(1,128)S(1)} all-gather(f32[1,1,2560]{2,1,0:T(1,128)S(1)} %bitcast.21), channel_id=1, replica_groups=mesh['x'=4,'core'=2,'z'=16,'y'=4] {'core'}, dimensions={0}, use_global_device_ids=true | all-gather | bytes 30720 | tf_op jit(solution)/shard_map/all_gather | solution.py:411
  27.4 1.3 %collective-permute-start.3 = (f32[1,5120]{1,0:T(1,128)S(1)}, f32[1,5120]{1,0:T(1,128)S(1)}, u32[]{:S(2)}, u32[]{:S(2)}) collective-permute-start(f32[1,5120]{1,0:T(1,128)S(1)} %bitcast.22), channel_id=1, source_target_pairs={{0,8},{4,12},{8,16},{12,20},{16,24},{20,28},{24,32},{28,36},{32,40... | collective-permute-start | bytes 61448 | tf_op jit(solution)/shard_map/ppermute | solution.py:416
  28.7 1.3 %collective-permute-start.2 = (f32[1,5120]{1,0:T(1,128)S(1)}, f32[1,5120]{1,0:T(1,128)}, u32[]{:S(2)}, u32[]{:S(2)}) collective-permute-start(f32[1,5120]{1,0:T(1,128)S(1)} %bitcast.23), channel_id=1, source_target_pairs={{0,4},{4,8},{8,12},{12,16},{16,20},{20,24},{24,28},{28,32},{32,36}... | collective-permute-start | bytes 61448 | tf_op jit(solution)/shard_map/ppermute | solution.py:416
  30.0 12.8 %all-to-all-start = ((f32[8,10,4,640]{3,2,1,0:T(4,128)}), f32[8,10,4,640]{3,2,1,0:T(4,128)S(1)}, u32[]{:S(2)}, u32[]{:S(2)}) async-start(f32[8,10,4,640]{3,2,1,0:T(4,128)} %get-tuple-element.21), calls=%async_computation | async-start | bytes 1638400 | tf_op jit(solution)/shard_map/all_to_all | solution.py:417
  42.7 0.0 collective-permute-done.3
  42.7 0.0 copy-start
  42.7 0.6 copy-done
  43.3 0.0 collective-permute-done.2
  43.3 0.8 %fusion.1 = f32[1,5120]{1,0:T(1,128)S(1)} fusion(f32[1,5120]{1,0:T(1,128)} %copy-done, f32[1,5120]{1,0:T(1,128)} %collective-permute-done.2, f32[1,5120]{1,0:T(1,128)S(1)} %bitcast.24, pred[]{:T(512)S(6)} %eq.6), kind=kLoop, calls=%fused_computation.2 | loop fusion | flops 15360 | bytes 81921 | tf_op jit(solution)/shard_map/add | solution.py:416
  44.1 11.2 %all-to-all-done = f32[8,10,4,640]{3,2,1,0:T(4,128)S(1)} async-done(((f32[8,10,4,640]{3,2,1,0:T(4,128)}), f32[8,10,4,640]{3,2,1,0:T(4,128)S(1)}, u32[]{:S(2)}, u32[]{:S(2)}) %all-to-all-start) | async-done | bytes 819232 | tf_op jit(solution)/shard_map/all_to_all | solution.py:417
  55.4 2.4 %all-gather.1 = f32[2,1,5120]{2,1,0:T(1,128)S(1)} all-gather(f32[1,1,5120]{2,1,0:T(1,128)S(1)} %bitcast.25), channel_id=1, replica_groups=mesh['x'=4,'core'=2,'z'=16,'y'=4] {'core'}, dimensions={0}, use_global_device_ids=true | all-gather | bytes 61440 | tf_op jit(solution)/shard_map/all_gather | solution.py:419
  57.8 0.2 broadcast_in_dim.17
  58.0 14.3 %all_to_all.10 = f32[32,1,2560]{2,1,0:T(1,128)S(1)} all-to-all(f32[32,1,2560]{2,1,0:T(1,128)S(1)} %broadcast_in_dim.17), channel_id=1, replica_groups=mesh['x'=4,'core'=2,'z'=16,'y'=4] {'core','y','x'}, dimensions={0} | all-to-all | bytes 655360 | tf_op jit(solution)/shard_map/all_to_all | solution.py:424
  72.2 2.8 %analyse.1 = f32[80,4,640]{2,1,0:T(4,128)} custom-call(f32[80,4,640]{2,1,0:T(4,128)S(1)} %bitcast.19, f32[2,4,4,1,2560]{4,3,2,1,0:T(1,128)S(1)} %bitcast.20, f32[8,256]{1,0:T(8,128)S(1)} %get-tuple-element.24.fields_ref, f32[256,2560]{1,0:T(8,128)S(1)} %get-tuple-element.25.weight_ref, f32[128,128]{1,0:T(8,128)S(1)} %get-tuple-element.26.cross_ref), custom_call_target="tpu_custom_call" | custom-call | tf_op jit(solution)/shard_map/analyse/pallas_call | solution.py:430
  (2 shorter events, 0.1 us)
Async XLA Ops:
  2.0 9.9 %collective-permute-start = (f32[81,2,640]{2,1,0:T(2,128)S(1)}, f32[81,2,640]{2,1,0:T(2,128)S(1)}, u32[]{:S(2)}, u32[]{:S(2)}) collective-permute-start(f32[81,2,640]{2,1,0:T(2,128)S(1)} %get-tuple-element.16), channel_id=1, source_target_pairs={{1,2},{3,4},{5,6},{7,8},{9,10},{11,12},{13,14},{15,16},{17,18},{19... | collective-permute-start | bytes 1244168 | tf_op jit(solution)/shard_map/ppermute | solution.py:348
  2.7 13.4 %collective-permute-start.1 = (f32[81,2,640]{2,1,0:T(2,128)S(1)}, f32[81,2,640]{2,1,0:T(2,128)S(1)}, u32[]{:S(2)}, u32[]{:S(2)}) collective-permute-start(f32[81,2,640]{2,1,0:T(2,128)S(1)} %get-tuple-element.17), channel_id=1, source_target_pairs={{0,1},{2,3},{4,5},{6,7},{8,9},{10,11},{12,13},{14,15},{16,17},{18,... | collective-permute-start | bytes 1244168 | tf_op jit(solution)/shard_map/ppermute | solution.py:348
  27.4 15.4 %collective-permute-start.3 = (f32[1,5120]{1,0:T(1,128)S(1)}, f32[1,5120]{1,0:T(1,128)S(1)}, u32[]{:S(2)}, u32[]{:S(2)}) collective-permute-start(f32[1,5120]{1,0:T(1,128)S(1)} %bitcast.22), channel_id=1, source_target_pairs={{0,8},{4,12},{8,16},{12,20},{16,24},{20,28},{24,32},{28,36},{32,40... | collective-permute-start | bytes 61448 | tf_op jit(solution)/shard_map/ppermute | solution.py:416
  28.7 14.7 %collective-permute-start.2 = (f32[1,5120]{1,0:T(1,128)S(1)}, f32[1,5120]{1,0:T(1,128)}, u32[]{:S(2)}, u32[]{:S(2)}) collective-permute-start(f32[1,5120]{1,0:T(1,128)S(1)} %bitcast.23), channel_id=1, source_target_pairs={{0,4},{4,8},{8,12},{12,16},{16,20},{20,24},{24,28},{28,32},{32,36}... | collective-permute-start | bytes 61448 | tf_op jit(solution)/shard_map/ppermute | solution.py:416
  30.0 25.4 %all-to-all-start = ((f32[8,10,4,640]{3,2,1,0:T(4,128)}), f32[8,10,4,640]{3,2,1,0:T(4,128)S(1)}, u32[]{:S(2)}, u32[]{:S(2)}) async-start(f32[8,10,4,640]{3,2,1,0:T(4,128)} %get-tuple-element.21), calls=%async_computation | async-start | bytes 1638400 | tf_op jit(solution)/shard_map/all_to_all | solution.py:417
  42.7 0.6 copy-start
